TPU v7x, 256 devices: a whole 4x4x8 slice. The times are simulated.
256 devices in a mesh: var: 8 (over x, z_hi), band: 32 (over z_lo, y, core).
Axes of the slice: x: 4, y: 4, z: 8 (z_hi: 2, z_lo: 4; z = z_hi * 4 + z_lo), core: 2. Of those that a mesh axis runs over, the one named last changes fastest.
Arguments:
- fields: bfloat16 [4, 80, 512, 1440], P(None, 'var', 'band'), may hold values from -6 to 6
- var_ids: int32 [80], P('var'), may hold values from 0 to 79, each once
- var_shift: float32 [80], replicated, may hold values from -4 to 4
- var_scale: float32 [80], replicated, may hold values from 0.3 to 3
- patch_weight: bfloat16 [80, 64, 1024], P('var'), may hold values from -1.25 to 1.25
- pos_table: float32 [16, 45, 1024], P(None, None, 'var'), may hold values from -5 to 5
- layer_norm_gain: float32 [1024], P('var'), may hold values from 0.5 to 1.5
- layer_norm_bias: float32 [1024], P('var'), may hold values from -2 to 2
- order: int32 [46080], P('band'), may hold values from 0 to 46079, as said below
- grad_out: bfloat16 [46080, 1024], P('band', 'var'), may hold values from -0.059814453 to 0.059814453
Outputs:
- embed: bfloat16 [46080, 1024], P('band', 'var')
- grad_weight: float32 [5120, 1024], P(('var', 'band'))
- grad_table: float32 [16, 45, 1024], P(None, None, 'var')
- grad_gain: float32 [1024], P('var')
- grad_bias: float32 [1024], P('var')
Inputs may be any that keep to these rules, and one draw needn't show every extreme that they name: `var_ids`: A permutation of the 80 variables. `order`: A permutation of the 46080 positions; each block of 1440 positions receives exactly 45 tokens from the 1440 tokens of every band.
All inputs are finite; a program needn't handle non-finite values.
Results may differ from a plain program's by a relative error of at most 0.011.
Values may be sent and summed in bfloat16 or wider, within the bound.
A program may use at most 128 MiB of HBM per device.

v0:
```python
import jax
import jax.numpy as jnp
from jax import lax
from jax.sharding import PartitionSpec as P

eps = 1e-05
stride_ratio = 4.0


def for_sending(x):
    return jax.tree.map(lambda a: a.astype(jnp.bfloat16) if a.dtype == jnp.float32 else a, x)


def blend_rows(lat_row, lon_col, tlat, tlon, first, count):
    u = jnp.clip((lat_row.astype(jnp.float32) + 0.5) / stride_ratio - 0.5, 0.0, tlat - 1.0)
    w = (lon_col.astype(jnp.float32) + 0.5) / stride_ratio - 0.5
    rows_at = (first + jnp.arange(count, dtype=jnp.int32)).astype(jnp.float32)
    lat_w = jnp.maximum(1.0 - jnp.abs(u[:, None] - rows_at[None, :]), 0.0)
    dist = jnp.abs(w[:, None] - jnp.arange(tlon).astype(jnp.float32)[None, :])
    dist = jnp.minimum(dist, tlon - dist)
    lon_w = jnp.maximum(1.0 - dist, 0.0)
    return (lat_w[:, :, None] * lon_w[:, None, :]).reshape(lat_row.shape[0], count * tlon)


def locate(source, tokens_band, rows_band, columns):
    inner = source % tokens_band
    band_of = source // tokens_band
    return (band_of * rows_band + inner // columns % rows_band, inner % columns)


def send_order(target, shards):
    count = target.shape[0]
    per = count // shards
    onehot = (target[:, None] == jnp.arange(shards)[None, :]).astype(jnp.int32)
    rank = jnp.sum((jnp.cumsum(onehot, 0) - onehot) * onehot, 1)
    where = target * per + rank
    return jnp.zeros((count,), jnp.int32).at[where].set(jnp.arange(count, dtype=jnp.int32))


def receive_order(slots):
    count = slots.shape[0]
    return jnp.zeros((count,), jnp.int32).at[slots].set(jnp.arange(count, dtype=jnp.int32))


def layer_normalize(prenorm_input, layer_norm_gain, layer_norm_bias, feature_width):
    sums, squares = lax.psum(
        (jnp.sum(prenorm_input, 1), jnp.sum(prenorm_input * prenorm_input, 1)), "var"
    )
    feature_mean = sums / feature_width
    inverse_deviation = lax.rsqrt(squares / feature_width - feature_mean * feature_mean + eps)
    normalized_input = (prenorm_input - feature_mean[:, None]) * inverse_deviation[:, None]
    return (
        normalized_input,
        inverse_deviation,
        (normalized_input * layer_norm_gain + layer_norm_bias).astype(jnp.bfloat16),
    )


def layer_normalize_backward(
    upstream_gradient, normalized_input, inverse_deviation, layer_norm_gain, feature_width
):
    scaled_values = upstream_gradient * layer_norm_gain
    grand_total, along_axis_name = lax.psum(
        (jnp.sum(scaled_values, 1), jnp.sum(scaled_values * normalized_input, 1)), "var"
    )
    preceding_gradient = inverse_deviation[:, None] * (
        scaled_values
        - (grand_total / feature_width)[:, None]
        - normalized_input * (along_axis_name / feature_width)[:, None]
    )
    return preceding_gradient.astype(jnp.bfloat16)


def on_device(
    fields,
    var_ids,
    var_shift,
    var_scale,
    patch_weight,
    pos_table,
    layer_norm_gain,
    layer_norm_bias,
    order,
    grad_out,
):
    samples, slots, lat_cells, lon_cells = fields.shape
    rows_band = lat_cells // 8
    columns = lon_cells // 8
    tb = samples * rows_band * columns
    shards = lax.axis_size("band")
    per = tb // shards
    feature_width = patch_weight.shape[2]
    part_width = pos_table.shape[2]
    tlat, tlon = (pos_table.shape[0], pos_table.shape[1])
    band = lax.axis_index("band")
    pick = (var_ids[:, None] == jnp.arange(var_shift.shape[0])[None, :]).astype(jnp.float32)
    shift = jnp.sum(pick * var_shift[None, :], 1)
    scale = jnp.sum(pick * var_scale[None, :], 1)
    normed = (
        (fields.astype(jnp.float32) - shift[None, :, None, None]) * scale[None, :, None, None]
    ).astype(jnp.bfloat16)
    patches = (
        normed.reshape(samples, slots, rows_band, 8, columns, 8)
        .transpose(0, 2, 4, 1, 3, 5)
        .reshape(tb, slots * 64)
    )
    flat_weight = patch_weight.reshape(slots * 64, feature_width)
    partial_value = jnp.dot(patches, flat_weight, preferred_element_type=jnp.float32).astype(
        jnp.bfloat16
    )
    local_ids = jnp.arange(tb, dtype=jnp.int32)
    tile_source = band * tb + local_ids
    tile_row, tile_col = locate(tile_source, tb, rows_band, columns)
    row_count = min(tlat, (rows_band + 2) // 4 + 2)
    lowest = jnp.clip(
        (band * rows_band).astype(jnp.float32) / stride_ratio + 0.5 / stride_ratio - 0.5,
        0.0,
        tlat - 1.0,
    )
    first_row = jnp.minimum(jnp.floor(lowest).astype(jnp.int32), tlat - row_count)
    tile_mix = blend_rows(tile_row, tile_col, tlat, tlon, first_row, row_count)
    table_rows = lax.dynamic_slice_in_dim(pos_table, first_row, row_count, 0).reshape(
        row_count * tlon, part_width
    )
    target = order // tb
    slot_in = order % tb
    outgoing = send_order(target, shards)
    info = jnp.stack([slot_in[outgoing], tile_source[outgoing]], 1).reshape(shards, per, 2)
    summed = lax.psum_scatter(
        partial_value.astype(jnp.float32), "var", scatter_dimension=1, tiled=True
    )
    prenorm_input = summed + jnp.dot(tile_mix, table_rows, precision=lax.Precision.HIGHEST)
    normalized_input, inverse_deviation, output_tile_block = layer_normalize(
        prenorm_input, layer_norm_gain, layer_norm_bias, feature_width
    )
    got, got_info = (
        lax.all_to_all(
            output_tile_block[outgoing].reshape(shards, per, part_width),
            "band",
            split_axis=0,
            concat_axis=0,
            tiled=True,
        ),
        lax.all_to_all(info, "band", split_axis=0, concat_axis=0, tiled=True),
    )
    got_info = got_info.reshape(tb, 2)
    placing = receive_order(got_info[:, 0])
    embed = got.reshape(tb, part_width)[placing]
    seq_source = got_info[:, 1][placing]
    returning = send_order(seq_source // tb, shards)
    back, back_slot = (
        lax.all_to_all(
            grad_out[returning].reshape(shards, per, part_width),
            "band",
            split_axis=0,
            concat_axis=0,
            tiled=True,
        ),
        lax.all_to_all(
            for_sending((seq_source % tb)[returning].reshape(shards, per)),
            "band",
            split_axis=0,
            concat_axis=0,
            tiled=True,
        ),
    )
    upstream_gradient = back.reshape(tb, part_width)[receive_order(back_slot.reshape(tb))].astype(
        jnp.float32
    )
    tile_portion = layer_normalize_backward(
        upstream_gradient, normalized_input, inverse_deviation, layer_norm_gain, feature_width
    )
    gain_product = jnp.sum(upstream_gradient * normalized_input, 0)
    bias_term = jnp.sum(upstream_gradient, 0)
    tile_full = lax.all_gather(tile_portion, "var", axis=1, tiled=True)
    rows_term = jnp.dot(
        tile_mix.T, tile_portion.astype(jnp.float32), precision=lax.Precision.HIGHEST
    )
    table_term = lax.dynamic_update_slice_in_dim(
        jnp.zeros((tlat, tlon, part_width), jnp.float32),
        rows_term.reshape(row_count, tlon, part_width),
        first_row,
        0,
    )
    grad_gain, grad_bias, grad_table = lax.psum((gain_product, bias_term, table_term), "band")
    grad_weight = lax.psum_scatter(
        jnp.dot(patches.T, tile_full, preferred_element_type=jnp.float32),
        "band",
        scatter_dimension=0,
        tiled=True,
    )
    return (embed, grad_weight, grad_table, grad_gain, grad_bias)


def solution(mesh):
    in_specs = (
        P(None, "var", "band", None),
        P("var"),
        P(),
        P(),
        P("var", None, None),
        P(None, None, "var"),
        P("var"),
        P("var"),
        P("band"),
        P("band", "var"),
    )
    out_specs = (
        P("band", "var"),
        P(("var", "band"), None),
        P(None, None, "var"),
        P("var"),
        P("var"),
    )
    return jax.shard_map(
        on_device, mesh=mesh, in_specs=in_specs, out_specs=out_specs, check_vma=False
    )
```

profile of v0, /device:TPU:32, one launch (start us, length us, event | category | flops | bytes accessed | tf_op | source)
XLA Modules:
  0.0 691.9 jit_solution(4008063558860355998)
XLA Ops:
  10.4 23.4 %reshape.294 = bf16[4,10,2,8,180,8]{5,4,3,2,1,0:T(8,128)(2,1)} reshape(bf16[4,10,16,1440]{3,2,1,0:T(8,128)(2,1)S(1)} %multiply_convert_fusion) | data formatting | bytes 3686400 | tf_op jit(solution)/shard_map/reshape | solution.py:103
  33.7 28.1 %copy.33 = bf16[4,2,180,10,8,8]{2,1,0,5,4,3:T(2,128)(2,1)} copy(bf16[4,2,180,10,8,8]{5,2,4,1,3,0:T(8,128)(2,1)} %bitcast.45) | data formatting | bytes 3686400 | tf_op jit(solution)/shard_map/transpose | solution.py:104
  61.9 7.9 %reshape.295 = bf16[1440,640]{0,1:T(8,128)(2,1)S(1)} reshape(bf16[4,2,180,10,8,8]{2,1,0,5,4,3:T(2,128)(2,1)} %copy.33) | data formatting | bytes 3686400 | tf_op jit(solution)/shard_map/reshape | solution.py:105
  69.8 5.0 fusion.1
  75.7 9.1 %reduce-window.14 = s32[32,12,128]{2,1,0:T(8,128)S(1)} reduce-window(s32[32,12,128]{2,1,0:T(8,128)S(1)} %reshape.307, s32[]{:T(128)} %constant.98.clone.1), window={size=1x1x128 pad=0_0x0_0x127_0}, to_apply=%region_7.8 | reduce-window | flops 6242304 | bytes 393220 | tf_op jit(solution)/shard_map/reduce-window
  85.5 7.6 %scatter_custom_fusion = s32[1440]{0:T(1024)S(1)} fusion(s32[1440]{0:T(1024)S(1)} %get-tuple-element.28, s32[1440]{0:T(1024)S(1)} %iota.43, s32[]{:T(128)} %constant.98.clone.1), kind=kCustom, calls=%fused_computation.129 | custom fusion | bytes 5764 | tf_op jit(solution)/shard_map/scatter | solution.py:37
  93.1 8.1 %gather_fusion.2 = s32[1440]{0:T(1024)S(1)} fusion(s32[1440]{0:T(1024)S(1)} %iota_add_fusion, s32[2048]{0:T(1024)S(1)} %pad_clamp_fusion.3), kind=kCustom, calls=%fused_computation.2 | custom fusion | bytes 17280 | tf_op jit(solution)/shard_map/gather | solution.py:128
  101.3 8.1 %gather_fusion.1 = s32[1440]{0:T(1024)S(1)} fusion(s32[1440]{0:T(1024)S(1)} %get-tuple-element.27, s32[2048]{0:T(1024)S(1)} %pad_clamp_fusion.3), kind=kCustom, calls=%fused_computation.1 | custom fusion | bytes 17280 | tf_op jit(solution)/shard_map/gather | solution.py:128
  110.2 8.8 %all-to-all-start.1 = ((s32[32,45,2]{1,2,0:T(2,128)}), s32[32,45,2]{1,2,0:T(2,128)S(1)}, u32[]{:S(2)}, u32[]{:S(2)}) async-start(s32[32,45,2]{1,2,0:T(2,128)} %copy.37), calls=%async_computation.2 | async-start | bytes 65536 | tf_op jit(solution)/shard_map/all_to_all | solution.py:144
  119.2 31.2 %all-to-all-done.1 = s32[32,45,2]{1,2,0:T(2,128)S(1)} async-done(((s32[32,45,2]{1,2,0:T(2,128)}), s32[32,45,2]{1,2,0:T(2,128)S(1)}, u32[]{:S(2)}, u32[]{:S(2)}) %all-to-all-start.1) | async-done | bytes 11552 | tf_op jit(solution)/shard_map/all_to_all | solution.py:144
  150.5 7.8 %scatter_custom_fusion.1 = s32[1440]{0:T(1024)S(1)} fusion(s32[1440]{0:T(1024)S(1)} %get-tuple-element.12, s32[1440]{0:T(1024)S(1)} %iota.44, s32[]{:T(128)} %constant.98.clone.1), kind=kCustom, calls=%fused_computation.127 | custom fusion | bytes 5764 | tf_op jit(solution)/shard_map/scatter | solution.py:42
  158.4 8.1 %gather_fusion.4 = s32[1440]{0:T(1024)S(1)} fusion(s32[1440]{0:T(1024)S(1)} %get-tuple-element.11, s32[2048]{0:T(1024)S(1)} %pad_clamp_fusion.2), kind=kCustom, calls=%fused_computation.4 | custom fusion | bytes 17280 | tf_op jit(solution)/shard_map/gather | solution.py:149
  166.6 9.1 %reduce-window.16 = s32[32,12,128]{2,1,0:T(8,128)S(1)} reduce-window(s32[32,12,128]{2,1,0:T(8,128)S(1)} %reshape.308, s32[]{:T(128)} %constant.98.clone.1), window={size=1x1x128 pad=0_0x0_0x127_0}, to_apply=%region_12.13 | reduce-window | flops 6242304 | bytes 393220 | tf_op jit(solution)/shard_map/reduce-window.2
  176.4 7.6 %scatter_custom_fusion.2 = s32[1440]{0:T(1024)S(1)} fusion(s32[1440]{0:T(1024)S(1)} %fusion.45, s32[1440]{0:T(1024)S(1)} %iota.45, s32[]{:T(128)} %constant.98.clone.1), kind=kCustom, calls=%fused_computation.125 | custom fusion | bytes 5764 | tf_op jit(solution)/shard_map/scatter | solution.py:37
  184.1 8.1 %gather_fusion.6 = s32[1440]{0:T(1024)S(1)} fusion(s32[1440]{0:T(1024)S(1)} %get-tuple-element.25, s32[2048]{0:T(1024)S(1)} %pad_clamp_fusion.1), kind=kCustom, calls=%fused_computation.6 | custom fusion | bytes 17280 | tf_op jit(solution)/shard_map/gather | solution.py:160
  192.9 9.2 %all-to-all-start.3 = ((s32[32,1,45]{2,1,0:T(1,128)}), s32[32,1,45]{2,1,0:T(1,128)S(1)}, u32[]{:S(2)}, u32[]{:S(2)}) async-start(s32[32,1,45]{2,1,0:T(1,128)} %all_to_all.18), calls=%async_computation.4 | async-start | bytes 32768 | tf_op jit(solution)/shard_map/all_to_all | solution.py:159
  202.1 3.4 gather_fusion.5
  206.4 10.9 %all-to-all-done.3 = s32[32,1,45]{2,1,0:T(1,128)S(1)} async-done(((s32[32,1,45]{2,1,0:T(1,128)}), s32[32,1,45]{2,1,0:T(1,128)S(1)}, u32[]{:S(2)}, u32[]{:S(2)}) %all-to-all-start.3) | async-done | bytes 5792 | tf_op jit(solution)/shard_map/all_to_all | solution.py:159
  217.3 5.0 all-to-all-start.2
  224.8 7.6 %scatter_custom_fusion.3 = s32[1440]{0:T(1024)S(1)} fusion(s32[1440]{0:T(1024)S(1)} %fusion.46, s32[1440]{0:T(1024)S(1)} %iota.46, s32[]{:T(128)} %constant.98.clone.1), kind=kCustom, calls=%fused_computation.131 | custom fusion | bytes 5764 | tf_op jit(solution)/shard_map/scatter | solution.py:42
  238.6 4.2 fusion.57
  242.8 46.5 %all-reduce.6 = (f32[1440]{0:T(1024)S(1)}, f32[1440]{0:T(1024)S(1)}) all-reduce(f32[1440]{0:T(1024)S(1)} %get-tuple-element.8, f32[1440]{0:T(1024)S(1)} %get-tuple-element.7), channel_id=1, replica_groups=mesh['var'=8,'band'=32] {'var'}, use_global_device_ids=true, to_apply=%region_6.7 | all-reduce | flops 2880 | bytes 23040 | tf_op jit(solution)/shard_map/psum | solution.py:46
  290.2 50.1 %all-reduce.5 = (f32[1440]{0:T(1024)S(1)}, f32[1440]{0:T(1024)S(1)}) all-reduce(f32[1440]{0:T(1024)S(1)} %get-tuple-element.6, f32[1440]{0:T(1024)S(1)} %get-tuple-element.9), channel_id=1, replica_groups=mesh['var'=8,'band'=32] {'var'}, use_global_device_ids=true, to_apply=%region_20.21 | all-reduce | flops 2880 | bytes 23040 | tf_op jit(solution)/shard_map/psum | solution.py:63
  346.7 5.0 all-to-all-start
  353.5 76.7 %all-gather.2.cloned.1.call-done = bf16[1440,1024]{1,0:T(8,128)(2,1)} async-done(((bf16[1440,128]{1,0:T(8,128)(2,1)}), bf16[1440,1024]{1,0:T(8,128)(2,1)}) %all-gather.2.cloned.1.call-update) | async-done | bytes 2949136 | tf_op jit(solution)/shard_map/all_gather | solution.py:175
  430.2 6.1 fusion.59
  436.3 69.0 %fusion = f32[24,1024]{1,0:T(8,128)S(1)} fusion(f32[640,1024]{1,0:T(8,128)} %fusion.59), kind=kCustom, calls=%all-reduce-scatter | all-reduce-scatter fusion | flops 786433 | bytes 2720768
  515.0 6.8 collective-permute-start.1
  521.8 4.8 collective-permute-start
  527.9 58.0 %all-reduce.4 = (f32[128]{0:T(128)}, f32[128]{0:T(128)}) all-reduce(f32[128]{0:T(128)S(1)} %get-tuple-element.5, f32[128]{0:T(128)S(1)} %get-tuple-element.10), channel_id=1, replica_groups=mesh['var'=8,'band'=32] {'band'}, use_global_device_ids=true, to_apply=%region_24.25 | all-reduce | flops 256 | bytes 2048 | tf_op jit(solution)/shard_map/psum | solution.py:185
  586.0 4.1 gather_fusion.3
  591.7 91.9 %all-reduce.9.cloned.1.call-done = f32[16,45,128]{2,0,1:T(8,128)} async-done(((f32[16,45,128]{2,0,1:T(8,128)}), f32[16,45,128]{2,0,1:T(8,128)}) %all-reduce.9.cloned.1.call-update) | async-done | bytes 368656 | tf_op jit(solution)/shard_map/psum | solution.py:185
  (119 shorter events, 39.6 us)
Async XLA Ops:
  7.2 62.6 %copy-start = (bf16[10,64,1024]{2,1,0:T(8,128)(2,1)S(1)}, bf16[10,64,1024]{2,1,0:T(8,128)(2,1)}, u32[]{:S(2)}) copy-start(bf16[10,64,1024]{2,1,0:T(8,128)(2,1)} %param.14) | copy-start | bytes 3932164
  7.2 231.5 %reduce-scatter.4.cloned.1.call-start = ((), (), s32[]{:S(2)}) async-start(), calls=%async_computation.5 | async-start | bytes 6635520 | tf_op jit(solution)/shard_map/reduce_scatter | solution.py:129
  69.8 5.0 copy-start.4
  74.8 0.7 copy-start.6
  110.2 40.2 %all-to-all-start.1 = ((s32[32,45,2]{1,2,0:T(2,128)}), s32[32,45,2]{1,2,0:T(2,128)S(1)}, u32[]{:S(2)}, u32[]{:S(2)}) async-start(s32[32,45,2]{1,2,0:T(2,128)} %copy.37), calls=%async_computation.2 | async-start | bytes 65536 | tf_op jit(solution)/shard_map/all_to_all | solution.py:144
  184.1 18.0 %copy-start.2 = (bf16[1440,128]{1,0:T(8,128)(2,1)S(1)}, bf16[1440,128]{1,0:T(8,128)(2,1)}, u32[]{:S(2)}) copy-start(bf16[1440,128]{1,0:T(8,128)(2,1)} %param.19) | copy-start | bytes 1105924
  192.9 24.4 %all-to-all-start.3 = ((s32[32,1,45]{2,1,0:T(1,128)}), s32[32,1,45]{2,1,0:T(1,128)S(1)}, u32[]{:S(2)}, u32[]{:S(2)}) async-start(s32[32,1,45]{2,1,0:T(1,128)} %all_to_all.18), calls=%async_computation.4 | async-start | bytes 32768 | tf_op jit(solution)/shard_map/all_to_all | solution.py:159
  217.3 17.8 %all-to-all-start.2 = ((bf16[32,45,128]{2,1,0:T(8,128)(2,1)}), bf16[32,45,128]{2,1,0:T(8,128)(2,1)S(1)}, u32[]{:S(2)}, u32[]{:S(2)}) async-start(bf16[32,45,128]{2,1,0:T(8,128)(2,1)} %reshape.304), calls=%async_computation.3 | async-start | bytes 786432 | tf_op jit(solution)/shard_map/all_to_all | solution.py:152
  222.3 207.9 %all-gather.2.cloned.1.call-start = ((), (), s32[]{:S(2)}) async-start(), calls=%async_computation.6 | async-start | bytes 3317760 | tf_op jit(solution)/shard_map/all_gather | solution.py:175
  235.2 54.1 %copy-start.7 = (f32[128]{0:T(128)S(1)}, f32[128]{0:T(128)}, u32[]{:S(2)}) copy-start(f32[128]{0:T(128)} %param.16) | copy-start | bytes 1540
  235.2 105.1 %copy-start.8 = (f32[128]{0:T(128)S(1)}, f32[128]{0:T(128)}, u32[]{:S(2)}) copy-start(f32[128]{0:T(128)} %param.17) | copy-start | bytes 1540
  342.5 9.3 %copy-start.3 = (bf16[1440,128]{1,0:T(8,128)(2,1)S(1)}, bf16[1440,128]{1,0:T(8,128)(2,1)}, u32[]{:S(2)}) copy-start(bf16[1440,128]{1,0:T(8,128)(2,1)} %get-tuple-element.23) | copy-start | bytes 1105924
  346.7 239.2 %all-to-all-start = ((bf16[32,45,128]{2,1,0:T(8,128)(2,1)}), bf16[32,45,128]{2,1,0:T(8,128)(2,1)S(1)}, u32[]{:S(2)}, u32[]{:S(2)}) async-start(bf16[32,45,128]{2,1,0:T(8,128)(2,1)} %reshape.299), calls=%async_computation.1 | async-start | bytes 786432 | tf_op jit(solution)/shard_map/all_to_all | solution.py:137
  351.7 332.0 %all-reduce.9.cloned.1.call-start = ((), (), s32[]{:S(2)}) async-start(), calls=%async_computation.7 | async-start | bytes 737280 | tf_op jit(solution)/shard_map/psum | solution.py:185
  352.7 0.8 copy-start.5
  436.3 90.3 %copy-start.9 = (u32[256]{0:T(256)S(1)}, u32[256]{0:T(256)}, u32[]{:S(2)}) copy-start(u32[256]{0:T(256)} %constant.123) | copy-start | bytes 3076
  505.4 16.4 %collective-permute-start.5 = (f32[4,1024]{1,0:T(4,128)S(1)}, f32[4,1024]{1,0:T(4,128)S(1)}, u32[]{:S(2)}, u32[]{:S(2)}) collective-permute-start(f32[4,1024]{1,0:T(4,128)S(1)} %slice.56), channel_id=1, source_target_pairs={{0,6},{1,7},{2,8},{3,9},{4,10},{5,11},{6,12},{7,13},{8,14},{9,15},... | collective-permute-start | bytes 49160
  507.3 82.8 %collective-permute-start.4 = (f32[24,1024]{1,0:T(8,128)S(1)}, f32[24,1024]{1,0:T(8,128)S(1)}, u32[]{:S(2)}, u32[]{:S(2)}) collective-permute-start(f32[24,1024]{1,0:T(8,128)S(1)} %fusion), channel_id=1, source_target_pairs={{0,5},{1,6},{2,7},{3,8},{4,9},{5,10},{6,11},{7,12},{8,13},{9,14},{... | collective-permute-start | bytes 294920
  509.2 80.9 %collective-permute-start.3 = (f32[24,1024]{1,0:T(8,128)S(1)}, f32[24,1024]{1,0:T(8,128)S(1)}, u32[]{:S(2)}, u32[]{:S(2)}) collective-permute-start(f32[24,1024]{1,0:T(8,128)S(1)} %fusion), channel_id=1, source_target_pairs={{0,4},{1,5},{2,6},{3,7},{4,8},{5,9},{6,10},{7,11},{8,12},{9,13},{1... | collective-permute-start | bytes 294920
  512.2 77.9 %collective-permute-start.2 = (f32[24,1024]{1,0:T(8,128)S(1)}, f32[24,1024]{1,0:T(8,128)S(1)}, u32[]{:S(2)}, u32[]{:S(2)}) collective-permute-start(f32[24,1024]{1,0:T(8,128)S(1)} %fusion), channel_id=1, source_target_pairs={{0,3},{1,4},{2,5},{3,6},{4,7},{5,8},{6,9},{7,10},{8,11},{9,12},{10... | collective-permute-start | bytes 294920
  515.0 75.1 %collective-permute-start.1 = (f32[24,1024]{1,0:T(8,128)S(1)}, f32[24,1024]{1,0:T(8,128)S(1)}, u32[]{:S(2)}, u32[]{:S(2)}) collective-permute-start(f32[24,1024]{1,0:T(8,128)S(1)} %fusion), channel_id=1, source_target_pairs={{0,2},{1,3},{2,4},{3,5},{4,6},{5,7},{6,8},{7,9},{8,10},{9,11},{10,... | collective-permute-start | bytes 294920
  521.8 68.3 %collective-permute-start = (f32[24,1024]{1,0:T(8,128)S(1)}, f32[24,1024]{1,0:T(8,128)S(1)}, u32[]{:S(2)}, u32[]{:S(2)}) collective-permute-start(f32[24,1024]{1,0:T(8,128)S(1)} %fusion), channel_id=1, source_target_pairs={{0,1},{1,2},{2,3},{3,4},{4,5},{5,6},{6,7},{7,8},{8,9},{9,10},{10,1... | collective-permute-start | bytes 294920
  585.9 99.5 %copy-start.1 = (bf16[10,64,1024]{2,1,0:T(8,128)(2,1)S(1)}, bf16[10,64,1024]{2,1,0:T(8,128)(2,1)}, u32[]{:S(2)}) copy-start(bf16[10,64,1024]{2,1,0:T(8,128)(2,1)} %param.14) | copy-start | bytes 3932164
Sparse Core Ops, SparseCore 0:
  75.0 153.6 reduce-scatter.3
  342.3 87.8 all-gather.1
  433.0 250.6 all-reduce.8
where the time goes:
time: 703 us; the launch traced here: 692 us
  blocking collectives  224 us (32%)
  waiting for transfers between devices  213 us (30%)
  local copies, waits for them, and re-layouts  149 us (21%)
  starting transfers between devices  49.3 us (7%)
  other arithmetic  25.8 us (4%)
  matrix products  15.9 us (2%)
  between operations  15.1 us (2%)
    psum x1, waiting for transfers between devices, on_device(): lax.psum((gain_product, bias_term, table_term), 'band')  91.9 us
    all_gather x1, waiting for transfers between devices, on_device(): tile_full = lax.all_gather(tile_portion, 'var', axis=1, tiled=True)  76.7 us
    unnamed x1, blocking collectives  69 us
    psum x1, blocking collectives, on_device(): lax.psum((gain_product, bias_term, table_term), 'band')  58 us
    psum x1, blocking collectives, layer_normalize_backward(): lax.psum((jnp.sum(scaled_values, 1), jnp.sum(scaled_values * normalized_i...  50.1 us
    psum x1, blocking collectives, layer_normalize(): lax.psum((jnp.sum(prenorm_input, 1), jnp.sum(prenorm_input * prenorm_inpu...  46.5 us
    all_to_all x1, waiting for transfers between devices, on_device(): lax.all_to_all(info, 'band', split_axis=0, concat_axis=0, tiled=True)  31.2 us
    transpose x1, local copies, waits for them, and re-layouts, on_device(): patches = normed.reshape(samples, slots, rows_band, 8, columns, 8).transp...  28.1 us
  transfers between devices with their start and end apart: 13, of which 5 were waited for; matrix products, arithmetic and copies ran while one was open for 26% of the time, Pallas kernels for 0%

commit v1 on v0

v1 whole, which is shorter than its diff:
```python
import functools

import jax
import jax.numpy as jnp
from jax import lax
from jax.experimental import pallas as pl
from jax.experimental.pallas import tpu as pltpu
from jax.sharding import PartitionSpec as P

EPS = 1e-05
T = 1536
LANES = 128
NB = 32
NV = 8
PER = 48
USED = 45
E = 1024
HALF = T // 2
PIECE = 256
PIECES = (0, 3, 1, 4, 2, 5)
F32 = jnp.float32
BF16 = jnp.bfloat16
HI = lax.Precision.HIGHEST


def iota(shape, dim):
    return lax.broadcasted_iota(jnp.int32, shape, dim)


def onehot(cond):
    return jnp.where(cond, 1.0, 0.0).astype(BF16)


def dot(a, b):
    return jnp.dot(a, b, preferred_element_type=F32)


def remote(src, dst, send, recv, v, b):
    return pltpu.make_async_remote_copy(
        src_ref=src,
        dst_ref=dst,
        send_sem=send,
        recv_sem=recv,
        device_id=(v, b),
        device_id_type=pl.DeviceIdType.MESH,
    )


class Place:
    def __init__(self):
        self.v = lax.axis_index("var")
        self.b = lax.axis_index("band")
        self.x = self.v // 2
        self.h = self.v % 2
        self.zl = self.b // 8
        self.y = (self.b // 2) % 4
        self.core = self.b % 2
        self.right = lax.rem(self.x + 1, 4) * 2 + self.h
        self.left = lax.rem(self.x + 3, 4) * 2 + self.h
        self.over = self.x * 2 + 1 - self.h

    def band_peer(self, k):
        return lax.rem(self.b + k, NB)

    def band_source(self, k):
        return lax.rem(self.b + NB - k, NB)


def greet(me, var_peers):
    barrier = pltpu.get_barrier_semaphore()

    @pl.loop(1, NB)
    def _(k):
        pl.semaphore_signal(
            barrier, inc=1, device_id=(me.v, me.band_peer(k)), device_id_type=pl.DeviceIdType.MESH
        )

    for peer in var_peers:
        pl.semaphore_signal(
            barrier, inc=1, device_id=(peer, me.b), device_id_type=pl.DeviceIdType.MESH
        )
    return lambda: pl.semaphore_wait(barrier, NB - 1 + len(var_peers))


def rows(i, n):
    return pl.ds(pl.multiple_of(i * n, n), n)


def exchange_start(me, src, dst, send, recv):
    @pl.loop(1, NB)
    def _(k):
        d = me.band_peer(k)
        remote(src(d), dst(me.b), send.at[d], recv.at[me.b], me.v, d).start()


def exchange_wait_recv(me, src, dst, send, recv):
    @pl.loop(1, NB)
    def _(k):
        s = me.band_source(k)
        remote(src(s), dst(s), send.at[s], recv.at[s], me.v, s).wait_recv()


def exchange_wait_send(me, src, dst, send, recv):
    @pl.loop(1, NB)
    def _(k):
        d = me.band_peer(k)
        remote(src(d), dst(d), send.at[d], recv.at[d], me.v, d).wait_send()


def mix_blocks(me, transposed):
    shape = (LANES, LANES)
    token = iota(shape, 1 if transposed else 0)
    cell = iota(shape, 0 if transposed else 1)
    second = cell >= 64
    j = jnp.where(second, cell - 64, cell)
    first = (me.b + 1) // 2 - 1

    def lat(p):
        u = jnp.clip(
            ((2 * me.b + p).astype(F32) + 0.5) / 4.0 - 0.5, 0.0, 15.0
        )
        w0 = jnp.maximum(1.0 - jnp.abs(u - first.astype(F32)), 0.0)
        w1 = jnp.maximum(1.0 - jnp.abs(u - (first + 1).astype(F32)), 0.0)
        return jnp.where(second, w1, w0)

    def lon(c):
        w = (c.astype(F32) + 0.5) / 4.0 - 0.5
        d = jnp.abs(w - j.astype(F32))
        d = jnp.minimum(d, 45.0 - d)
        return jnp.where(j < 45, jnp.maximum(1.0 - d, 0.0), 0.0)

    lat0, lat1 = lat(0), lat(1)
    low = lon(token)
    end0 = jnp.where(token < 52, lat0 * lon(token + 128), 0.0)
    end1 = jnp.where(
        jnp.logical_and(token >= 52, token < 104), lat1 * lon(token + 76), 0.0
    )
    return [(m).astype(BF16) for m in (lat0 * low, lat1 * low, end0 + end1)]


def which_mix(tile):
    return tile % 2 if tile < 8 else 2


def forward_kernel(
    ids, shift, scale, fields, weight, table, places, gout,
    pre, cot, xb, posrow, slotrow,
    cols, poscol, rhi, rlo, info, got_info, slotcol, gpad, cot_out, cot_in,
    xn, sel, sel_end, perm, permb, xt, xrow, wq, part, fwd, from_left, from_right,
    zout, zin, window,
    info_s, info_r, cot_s, cot_r, xs, fwd_r, left_r, right_r, z_s, z_r,
):
    me = Place()
    wait_barrier = greet(me, (me.right, me.left, me.over))

    r8 = places[...]
    cols[...] = jnp.concatenate([r8, jnp.zeros((120, T), F32)], 0).T
    lane = iota((LANES, LANES), 1)
    lanef = lane.astype(F32)
    below = onehot(iota((LANES, LANES), 0) > lane)
    target_row = r8[0:1, :]
    to_shard = onehot(iota((NB, T), 0).astype(F32) == target_row)
    carry = jnp.zeros((1, LANES), F32)
    for i in range(T // LANES):
        sl = slice(i * LANES, (i + 1) * LANES)
        target = cols[sl, 0:1]
        hot = jnp.where(target == lanef, 1.0, 0.0)
        before = dot(below, hot.astype(BF16)) + carry
        rank = jnp.sum(hot * before, 1, keepdims=True)
        carry = carry + jnp.sum(hot, 0, keepdims=True)
        at = jnp.where(rank == lanef, 1.0, 0.0)
        rhi[sl, :] = (at * cols[sl, 1:2]).astype(BF16)
        rlo[sl, :] = (at * cols[sl, 2:3]).astype(BF16)
        pos = jnp.broadcast_to(target * PER + rank, (LANES, LANES))
        poscol[sl, :] = pos
        posrow[:, sl] = pos.T[0:8]
    slots = dot(to_shard, rhi[...]) * 32.0 + dot(to_shard, rlo[...])
    slots = jnp.where(iota((NB, LANES), 1) < USED, slots, -1.0)
    for d in range(NB):
        info[d] = jnp.broadcast_to(slots[d : d + 1], (8, LANES))

    wait_barrier()
    info_args = (me, lambda d: info.at[d], lambda s: got_info.at[s], info_s, info_r)
    exchange_start(*info_args)
    got_info[pl.ds(me.b, 1)] = info[pl.ds(me.b, 1)]

    xn[:, :, :, 1408:1536] = jnp.zeros((2, 4, 80, 128), BF16)

    @pl.loop(0, 4)
    def _(s):
        for pair in range(5):
            halves = []
            for k in (2 * pair, 2 * pair + 1):
                at = ids[k]
                halves.append((fields[s, k].astype(F32) - shift[at]) * scale[at])
            for p in range(2):
                both = jnp.concatenate([n[8 * p : 8 * p + 8] for n in halves], 0)
                xn[p, s, 16 * pair : 16 * pair + 16, 0:1440] = both.astype(BF16)

    @pl.loop(0, 8)
    def _(i):
        n = iota((LANES, E), 1)
        k = iota((LANES, E), 0) + i * LANES
        sel[rows(i, LANES), :] = onehot(k == (n & 127) * 8 + (n >> 7))

    @pl.loop(0, 4)
    def _(i):
        n = iota((LANES, E), 1)
        k = iota((LANES, E), 0) + i * LANES
        sel_end[rows(i, LANES), :] = onehot(k == ((n & 127) - 52) * 8 + (n >> 7))

    @pl.loop(0, 4)
    def _(i):
        out = pl.ds(pl.multiple_of(i * 256, 256), 256)
        low = dot(xn[...].reshape(640, T)[:, 0:1024], sel[:, out]).astype(BF16)
        end = (
            dot(xn[0].reshape(320, T)[:, 1024:1536], sel[0:512, out])
            + dot(xn[1].reshape(320, T)[:, 1024:1536], sel_end[:, out])
        ).astype(BF16)
        for q in range(2):
            at = pl.ds(pl.multiple_of((2 * i + q) * 80, 80), 80)
            lanes = slice(q * 128, q * 128 + 128)
            for s in range(4):
                for p in range(2):
                    tile = 2 * s + p
                    first = (p * 4 + s) * 80
                    xt[at, tile * 128 : tile * 128 + 128] = low[first : first + 80, lanes]
                xt[at, 1024 + s * 128 : 1152 + s * 128] = end[s * 80 : s * 80 + 80, lanes]

    eye = onehot(iota((LANES, LANES), 0) == lane)

    @pl.loop(0, T // LANES)
    def _(i):
        xrow[rows(i, LANES), :] = lax.dot_general(
            eye, xt[:, rows(i, LANES)], (((1,), (1,)), ((), ())), preferred_element_type=F32
        ).astype(BF16)

    n = iota((80, 640), 1)
    g = iota((80, 640), 0)
    for dx in range(8):
        perm[dx * 80 : dx * 80 + 80, :] = onehot(n == g * 8 + dx)

    def quarter(j, ahead):
        at = lax.rem(me.x + ahead, 4)
        wq[...] = dot(perm[...], weight[:, pl.ds(pl.multiple_of(at * 256, 256), 256)]).astype(BF16)

        @pl.loop(0, T // PIECE)
        def _(i):
            part[j, rows(i, PIECE), :] = dot(xrow[rows(i, PIECE), :], wq[...]).astype(BF16)

    def piece(ref, p):
        return ref.at[pl.ds(p * PIECE, PIECE)]

    sends = []

    def send(copy):
        copy.start()
        sends.append(copy)

    quarter(0, 2)
    for p in PIECES:
        send(remote(piece(part.at[0], p), piece(fwd, p), xs.at[p], fwd_r.at[p],
                    me.right if p < 3 else me.left, me.b))
    quarter(1, 1)
    for p in (3, 4, 5):
        send(remote(piece(part.at[1], p), piece(from_left, p), xs.at[6 + p], left_r.at[p],
                    me.right, me.b))
    quarter(2, 3)
    for p in (0, 1, 2):
        send(remote(piece(part.at[2], p), piece(from_right, p), xs.at[6 + p], right_r.at[p],
                    me.left, me.b))

    exchange_wait_recv(*info_args)
    gpad[1440:T, :] = jnp.zeros((T - 1440, LANES), BF16)
    gpad[0:1440, :] = gout[...]
    same = iota((PER, LANES), 0) == iota((PER, LANES), 1)

    @pl.loop(0, NB)
    def _(s):
        asked = jnp.broadcast_to(got_info[s][0:1], (PER, LANES))
        at = jnp.sum(jnp.where(same, asked, 0.0), 1, keepdims=True)
        slotcol[rows(s, PER), :] = jnp.broadcast_to(at, (PER, LANES))

    wide = iota((384, T), 1).astype(F32)

    @pl.loop(0, 4)
    def _(i):
        hot = onehot(slotcol[rows(i, 384), 0:1] == wide)
        cot_out[rows(i, 384), :] = dot(hot, gpad[...]).astype(BF16)

    cot_args = (
        me,
        lambda d: cot_out.at[rows(d, PER)],
        lambda s: cot_in.at[rows(s, PER)],
        cot_s,
        cot_r,
    )
    exchange_start(*cot_args)
    cot_in[rows(me.b, PER), :] = cot_out[rows(me.b, PER), :]
    for i in range(T // LANES):
        sl = slice(i * LANES, (i + 1) * LANES)
        slotrow[:, sl] = slotcol[sl, :].T[0:8]

    quarter(3, 0)

    for p in PIECES:
        if p < 3:
            remote(piece(part.at[0], p), piece(fwd, p), xs.at[p], fwd_r.at[p],
                   me.left, me.b).wait_recv()
            sl = slice(p * PIECE, (p + 1) * PIECE)
            part[1, sl, :] = (part[1, sl, :].astype(F32) + fwd[sl, :].astype(F32)).astype(BF16)
            send(remote(piece(part.at[1], p), piece(from_left, p), xs.at[12 + p], left_r.at[p],
                        me.right, me.b))
        else:
            remote(piece(part.at[0], p), piece(fwd, p), xs.at[p], fwd_r.at[p],
                   me.right, me.b).wait_recv()
            sl = slice(p * PIECE, (p + 1) * PIECE)
            part[2, sl, :] = (part[2, sl, :].astype(F32) + fwd[sl, :].astype(F32)).astype(BF16)
            send(remote(piece(part.at[2], p), piece(from_right, p), xs.at[12 + p], right_r.at[p],
                        me.left, me.b))

    r = iota((640, 1), 0)

    def steps(a, size, count):
        at = jnp.zeros_like(a)
        for i in range(1, count):
            at = at + jnp.where(a >= i * size, 1, 0)
        return at

    core = steps(r, 320, 2)
    r = r - 320 * core
    y = steps(r, 80, 4)
    r = r - 80 * y
    zl = steps(r, 20, 4)
    n = 20 * (zl * 8 + y * 2 + core) + r - 20 * zl
    permb[...] = onehot(iota((640, 640), 1) == (n & 7) * 80 + (n >> 3))

    @pl.loop(0, T // PIECE)
    def _(i):
        xb[:, rows(i, PIECE)] = dot(permb[...], xt[:, rows(i, PIECE)]).astype(BF16)

    first = (me.b + 1) // 2 - 1
    window[...] = jnp.zeros((LANES, LANES), F32)
    window[0:45, :] = table[jnp.maximum(first, 0)]
    window[64:109, :] = table[jnp.minimum(first + 1, 15)]
    position = [
        jnp.dot(m.astype(F32), window[...], precision=HI, preferred_element_type=F32)
        for m in mix_blocks(me, False)
    ]

    for p in PIECES:
        src = part.at[1]
        remote(piece(src, p), piece(from_left, p), xs.at[p], left_r.at[p], me.left, me.b).wait_recv()
        remote(piece(src, p), piece(from_right, p), xs.at[p], right_r.at[p], me.right, me.b).wait_recv()
        sl = slice(p * PIECE, (p + 1) * PIECE)
        total = (
            part[3, sl, :].astype(F32) + from_left[sl, :].astype(F32)
        ) + from_right[sl, :].astype(F32)
        mine = jnp.where(me.h == 0, total[:, 0:128], total[:, 128:256])
        other = jnp.where(me.h == 0, total[:, 128:256], total[:, 0:128])
        zout[sl, :] = other.astype(BF16)
        send(remote(piece(zout, p), piece(zin, p), z_s.at[p], z_r.at[p], me.over, me.b))
        pre[sl, :] = mine + jnp.concatenate(
            [position[which_mix(2 * p)], position[which_mix(2 * p + 1)]], 0
        )

    exchange_wait_recv(*cot_args)

    @pl.loop(0, 4)
    def _(i):
        hot = onehot(poscol[rows(i, 384), 0:1] == wide)
        cot[rows(i, 384), :] = dot(hot, cot_in[...]).astype(BF16)

    for p in PIECES:
        remote(piece(zout, p), piece(zin, p), z_s.at[p], z_r.at[p], me.over, me.b).wait_recv()
        sl = slice(p * PIECE, (p + 1) * PIECE)
        pre[sl, :] = pre[sl, :] + zin[sl, :].astype(F32)

    for copy in sends:
        copy.wait_send()
    exchange_wait_send(*info_args)
    exchange_wait_send(*cot_args)


def backward_kernel(
    pre, cot, xb, posrow, slotrow, gain_in, bias_in,
    embed, grad_weight, grad_table, grad_gain, grad_bias,
    stat, packed, got_stat, statcol, emb, emb_out, emb_in, dg,
    core_out, core_in, gw, y_out, y_in, zl_out, zl_in,
    outer, outer_in, inner, chip, chip_in, tables,
    stat_s, stat_r, emb_s, emb_r, dz_s, dz_r, dx_s, dr_r, dl_r, df_s, df_r,
    core_s, core_r, y_s, y_r, zl_s, zl_r, t_s, t_r, tab_s, tab_r,
):
    me = Place()
    var_peers = [lax.rem(me.v + k, NV) for k in range(1, NV)]
    wait_barrier = greet(me, var_peers)
    gain = gain_in[...]
    bias = bias_in[...]
    sends = []

    def send(copy):
        copy.start()
        sends.append(copy)

    lane = iota((PIECE, LANES), 1)
    for p in range(T // PIECE):
        sl = slice(p * PIECE, (p + 1) * PIECE)
        a = pre[sl, :]
        g = cot[sl, :].astype(F32) * gain
        sums = [jnp.sum(q, 1, keepdims=True) for q in (a, a * a, g, g * a)]
        base = 0 if p < 3 else 4
        block = jnp.zeros((PIECE, LANES), F32)
        for k in range(4):
            block = jnp.where(lane == base + k, sums[k], block)
        stat[sl, :] = block
    flat = stat[...].T
    packed[...] = flat[0:8, 0:HALF] + flat[0:8, HALF:T]
    wait_barrier()
    for k in range(1, NV):
        send(remote(packed, got_stat.at[me.v], stat_s.at[k - 1], stat_r.at[me.v],
                    var_peers[k - 1], me.b))
    got_stat[pl.ds(me.v, 1)] = packed[...][None]
    for k in range(1, NV):
        src = lax.rem(me.v + NV - k, NV)
        remote(packed, got_stat.at[src], stat_s.at[k - 1], stat_r.at[src], src, me.b).wait_recv()
    total = got_stat[0]
    for k in range(1, NV):
        total = total + got_stat[k]
    statcol[...] = jnp.concatenate(
        [jnp.concatenate([total, total], 1), jnp.zeros((120, T), F32)], 0
    ).T

    own = dg.at[0, me.h]
    gain_sum = jnp.zeros((1, LANES), F32)
    bias_sum = jnp.zeros((1, LANES), F32)
    for half in range(2):
        for p in range(3 * half, 3 * half + 3):
            sl = slice(p * PIECE, (p + 1) * PIECE)
            s1, s2, sg, sq = [statcol[sl, 4 * half + k : 4 * half + k + 1] for k in range(4)]
            mean = s1 / E
            inv = lax.rsqrt(s2 / E - mean * mean + EPS)
            xhat = (pre[sl, :] - mean) * inv
            up = cot[sl, :].astype(F32)
            emb[sl, :] = (xhat * gain + bias).astype(BF16)
            along = inv * (sq - mean * sg) / E
            d = inv * (up * gain - sg / E - xhat * along)
            own[sl, :] = d.astype(BF16)
            gain_sum = gain_sum + jnp.sum(up * xhat, 0, keepdims=True)
            bias_sum = bias_sum + jnp.sum(up, 0, keepdims=True)
        hs = pl.ds(half * HALF, HALF)
        send(remote(own.at[hs], own.at[hs], dz_s.at[half], dz_r.at[half], me.over, me.b))
        at = 2 * me.h + half
        send(remote(own.at[hs], dg.at[1, me.h, hs], dx_s.at[half], dr_r.at[at], me.right, me.b))
        send(remote(own.at[hs], dg.at[2, me.h, hs], dx_s.at[2 + half], dl_r.at[at], me.left, me.b))

    tall = iota((384, T), 0).astype(F32)

    @pl.loop(0, 4)
    def _(i):
        hot = onehot(posrow[0:1, :] == tall + (i * 384).astype(F32))
        emb_out[rows(i, 384), :] = dot(hot, emb[...]).astype(BF16)

    emb_args = (
        me,
        lambda d: emb_out.at[rows(d, PER)],
        lambda s: emb_in.at[rows(s, PER)],
        emb_s,
        emb_r,
    )
    exchange_start(*emb_args)
    emb_in[rows(me.b, PER), :] = emb_out[rows(me.b, PER), :]

    mixes = mix_blocks(me, True)
    rows_term = jnp.zeros((LANES, LANES), F32)
    for i in range(T // LANES):
        rows_term = rows_term + dot(mixes[which_mix(i)], own[i * LANES : (i + 1) * LANES, :])
    even = me.core == 0
    outer[...] = jnp.where(even, rows_term[0:48], rows_term[64:112])
    at = iota((48, LANES), 0)
    inner[...] = jnp.where(even, rows_term[64:112], rows_term[0:48])
    across = jnp.where(even, lax.rem(me.b + NB - 1, NB), lax.rem(me.b + 1, NB))
    mate = jnp.where(even, me.b + 1, me.b - 1)
    outer_copy = remote(outer, outer_in, t_s.at[0], t_r.at[0], me.v, across)
    send(outer_copy)

    over = dg.at[0, 1 - me.h]
    for half in range(2):
        hs = pl.ds(half * HALF, HALF)
        remote(own.at[hs], over.at[hs], dz_s.at[half], dz_r.at[half], me.over, me.b).wait_recv()
        at2 = 2 * (1 - me.h) + half
        send(remote(over.at[hs], dg.at[1, 1 - me.h, hs], dx_s.at[4 + half], dr_r.at[at2],
                    me.right, me.b))
        send(remote(over.at[hs], dg.at[2, 1 - me.h, hs], dx_s.at[6 + half], dl_r.at[at2],
                    me.left, me.b))

    outer_copy.wait_recv()
    both = inner[...] + outer_in[...]
    both = jnp.where(at == 45, gain_sum, jnp.where(at == 46, bias_sum, both))
    chip[...] = both
    chip_copy = remote(chip, chip_in, t_s.at[1], t_r.at[1], me.v, mate)
    send(chip_copy)

    mate_core = 1 - me.core

    def multiply(c):
        left = xb
        right = jnp.concatenate([dg[c, 0], dg[c, 1]], 1)
        theirs = left[pl.ds(pl.multiple_of(mate_core * 320, 320), 320), :]
        core_out[c] = dot(theirs, right).astype(BF16)
        send(remote(core_out.at[c], core_in.at[c], core_s.at[c], core_r.at[c], me.v, mate))
        mine = left[pl.ds(pl.multiple_of(me.core * 320, 320), 320), :]
        gw[c] = dot(mine, right)

    def over_y(c):
        remote(core_out.at[c], core_in.at[c], core_s.at[c], core_r.at[c], me.v, mate).wait_recv()
        y_out[c] = (gw[c] + core_in[c].astype(F32)).astype(BF16)
        for k in range(1, 4):
            to = lax.rem(me.y + k, 4)
            src = y_out.at[c, rows(to, 80)]
            send(remote(src, y_in.at[c, k - 1], y_s.at[c, k - 1], y_r.at[c, k - 1],
                        me.v, me.zl * 8 + to * 2 + me.core))

    spread_r = iota((128, 80), 0)
    spread_c = iota((128, 80), 1)
    group = spread_r >> 5
    inside = spread_r & 31
    spread = onehot(
        jnp.logical_and(inside < 20, spread_c == group * 20 + inside)
    )

    def over_z(c):
        total = y_out[c, rows(me.y, 80), :].astype(F32)
        for k in range(1, 4):
            src = lax.rem(me.y + 4 - k, 4)
            remote(y_out.at[c, rows(src, 80)], y_in.at[c, k - 1], y_s.at[c, k - 1],
                   y_r.at[c, k - 1], me.v, me.zl * 8 + src * 2 + me.core).wait_recv()
            total = total + y_in[c, k - 1].astype(F32)
        zl_out[c] = dot(spread, total.astype(BF16)).astype(BF16)
        for k in range(1, 4):
            to = lax.rem(me.zl + k, 4)
            send(remote(zl_out.at[c, rows(to, 32)], zl_in.at[c, k - 1], zl_s.at[c, k - 1],
                        zl_r.at[c, k - 1], me.v, to * 8 + me.y * 2 + me.core))

    ahead = (0, 3, 1, 2)

    def finish(c):
        total = zl_out[c, rows(me.zl, 32), :].astype(F32)
        for k in range(1, 4):
            src = lax.rem(me.zl + 4 - k, 4)
            remote(zl_out.at[c, rows(src, 32)], zl_in.at[c, k - 1], zl_s.at[c, k - 1],
                   zl_r.at[c, k - 1], me.v, src * 8 + me.y * 2 + me.core).wait_recv()
            total = total + zl_in[c, k - 1].astype(F32)
        x = lax.rem(me.x + ahead[c], 4)
        grad_weight[:, pl.ds(pl.multiple_of(x * 256, 256), 256)] = total[0:20]

    def await_x(c):
        for hh in range(2):
            for half in range(2):
                hs = pl.ds(half * HALF, HALF)
                src = dg.at[0, hh, hs]
                if c == 1:
                    remote(src, dg.at[1, hh, hs], dx_s.at[0], dr_r.at[2 * hh + half],
                           me.left, me.b).wait_recv()
                    if half == 0:
                        send(remote(dg.at[1, hh, hs], dg.at[3, hh, hs], df_s.at[2 * hh],
                                    df_r.at[2 * hh], me.right, me.b))
                elif c == 2:
                    remote(src, dg.at[2, hh, hs], dx_s.at[0], dl_r.at[2 * hh + half],
                           me.right, me.b).wait_recv()
                    if half == 1:
                        send(remote(dg.at[2, hh, hs], dg.at[3, hh, hs], df_s.at[2 * hh + 1],
                                    df_r.at[2 * hh + 1], me.left, me.b))
                else:
                    remote(src, dg.at[3, hh, hs], dx_s.at[0], df_r.at[2 * hh + half],
                           me.left, me.b).wait_recv()

    multiply(0)

    chip_copy.wait_recv()
    m = me.zl * 4 + me.y
    tables[pl.ds(m, 1)] = (chip[...] + chip_in[...])[None]
    for k in range(1, 16):
        to = lax.rem(m + k, 16)
        send(remote(tables.at[m], tables.at[m], tab_s.at[k - 1], tab_r.at[m],
                    me.v, to * 2 + me.core))

    await_x(1)
    await_x(2)
    multiply(1)
    over_y(0)
    multiply(2)
    over_y(1)
    over_z(0)

    exchange_wait_recv(*emb_args)

    @pl.loop(0, 3)
    def _(i):
        hot = onehot(slotrow[0:1, :] == iota((480, T), 0).astype(F32) + (i * 480).astype(F32))
        embed[rows(i, 480), :] = dot(hot, emb_in[...]).astype(BF16)

    over_y(2)
    over_z(1)
    await_x(3)
    multiply(3)
    over_z(2)
    finish(0)
    over_y(3)
    finish(1)

    for k in range(1, 16):
        src = lax.rem(m + 16 - k, 16)
        remote(tables.at[src], tables.at[src], tab_s.at[k - 1], tab_r.at[src],
               me.v, src * 2 + me.core).wait_recv()
    gain_total = jnp.zeros((1, LANES), F32)
    bias_total = jnp.zeros((1, LANES), F32)
    for i in range(16):
        grad_table[i] = tables[i, 0:45, :]
        gain_total = gain_total + tables[i, 45:46, :]
        bias_total = bias_total + tables[i, 46:47, :]
    grad_gain[...] = gain_total
    grad_bias[...] = bias_total

    over_z(3)
    finish(2)
    finish(3)
    for copy in sends:
        copy.wait_send()
    exchange_wait_send(*emb_args)


def dma(*shape):
    return pltpu.SemaphoreType.DMA(shape)


def vmem(shape, dtype=BF16):
    return pltpu.VMEM(shape, dtype)


def on_device(
    fields, var_ids, var_shift, var_scale, patch_weight, pos_table,
    layer_norm_gain, layer_norm_bias, order, grad_out,
):
    token = order.reshape(8, 180)
    target = token // 1440
    slot = token % 1440
    three = jnp.stack([target, slot // 32, slot % 32], 0).astype(F32)
    ends = jnp.pad(
        three[:, :, 128:].reshape(3, 4, 104), ((0, 0), (0, 0), (0, 24)), constant_values=99.0
    )
    places = jnp.concatenate([three[:, :, :128].reshape(3, 1024), ends.reshape(3, 512)], 1)
    places = jnp.pad(places, ((0, 5), (0, 0)))

    here = pl.BlockSpec(memory_space=pltpu.VMEM)
    scalars = pl.BlockSpec(memory_space=pltpu.SMEM)
    params = functools.partial(
        pltpu.CompilerParams, has_side_effects=True, vmem_limit_bytes=56 * 1024 * 1024
    )
    shape = jax.ShapeDtypeStruct
    pre, cot, xb, posrow, slotrow = pl.pallas_call(
        forward_kernel,
        out_shape=(
            shape((T, LANES), F32),
            shape((T, LANES), BF16),
            shape((640, T), BF16),
            shape((8, T), F32),
            shape((8, T), F32),
        ),
        in_specs=[scalars] * 3 + [here] * 5,
        out_specs=(here,) * 5,
        scratch_shapes=[
            vmem((T, LANES), F32), vmem((T, LANES), F32), vmem((T, LANES)), vmem((T, LANES)),
            vmem((NB, 8, LANES), F32), vmem((NB, 8, LANES), F32), vmem((T, LANES), F32),
            vmem((T, LANES)), vmem((T, LANES)), vmem((T, LANES)),
            vmem((2, 4, 80, T)), vmem((E, E)), vmem((512, E)),
            vmem((640, 640)), vmem((640, 640)), vmem((640, T)), vmem((T, 640)),
            vmem((640, 256)), vmem((4, T, 256)), vmem((T, 256)), vmem((T, 256)), vmem((T, 256)),
            vmem((T, LANES)), vmem((T, LANES)), vmem((LANES, LANES), F32),
            dma(NB), dma(NB), dma(NB), dma(NB), dma(18), dma(6), dma(6), dma(6), dma(6), dma(6),
        ],
        compiler_params=params(collective_id=0),
        name="forward",
    )(
        var_ids, var_shift, var_scale, fields, patch_weight.reshape(640, E), pos_table,
        places, grad_out,
    )
    embed, grad_weight, grad_table, grad_gain, grad_bias = pl.pallas_call(
        backward_kernel,
        out_shape=(
            shape((1440, LANES), BF16),
            shape((20, E), F32),
            shape((16, 45, LANES), F32),
            shape((1, LANES), F32),
            shape((1, LANES), F32),
        ),
        in_specs=[here] * 7,
        out_specs=(here,) * 5,
        scratch_shapes=[
            vmem((T, LANES), F32), vmem((8, HALF), F32), vmem((NV, 8, HALF), F32),
            vmem((T, LANES), F32), vmem((T, LANES)), vmem((T, LANES)), vmem((T, LANES)),
            vmem((4, 2, T, LANES)),
            vmem((4, 320, 256)), vmem((4, 320, 256)), vmem((4, 320, 256), F32),
            vmem((4, 320, 256)), vmem((4, 3, 80, 256)),
            vmem((4, 128, 256)), vmem((4, 3, 32, 256)),
            vmem((48, LANES), F32), vmem((48, LANES), F32), vmem((48, LANES), F32),
            vmem((48, LANES), F32), vmem((48, LANES), F32), vmem((16, 48, LANES), F32),
            dma(7), dma(8), dma(NB), dma(NB), dma(2), dma(2), dma(8), dma(4), dma(4),
            dma(4), dma(4), dma(4), dma(4), dma(4, 3), dma(4, 3), dma(4, 3), dma(4, 3),
            dma(2), dma(2), dma(15), dma(16),
        ],
        compiler_params=params(collective_id=1),
        name="backward",
    )(
        pre, cot, xb, posrow, slotrow,
        layer_norm_gain.reshape(1, LANES), layer_norm_bias.reshape(1, LANES),
    )
    return embed, grad_weight, grad_table, grad_gain.reshape(LANES), grad_bias.reshape(LANES)


def solution(mesh):
    in_specs = (
        P(None, "var", "band", None),
        P("var"),
        P(),
        P(),
        P("var", None, None),
        P(None, None, "var"),
        P("var"),
        P("var"),
        P("band"),
        P("band", "var"),
    )
    out_specs = (
        P("band", "var"),
        P(("var", "band"), None),
        P(None, None, "var"),
        P("var"),
        P("var"),
    )
    return jax.shard_map(
        on_device, mesh=mesh, in_specs=in_specs, out_specs=out_specs, check_vma=False
    )
```

time: 703 us -> 149 us (0.21); the launches traced: 692 us -> 148 us
  blocking collectives: 224 us -> 0 us
  waiting for transfers between devices: 213 us -> 0 us
  local copies, waits for them, and re-layouts: 149 us -> 9.59 us
  Pallas kernels: 0 us -> 136 us
  starting transfers between devices: 49.3 us -> 0 us
  other arithmetic: 25.8 us -> 2.07 us
  matrix products: 15.9 us -> 0 us
  between operations: 15.1 us -> 0.7 us
    psum x3 -> x0, blocking collectives: 155 us -> none  [the longest x1 58 us: on_device(): lax.psum((gain_product, bias_term, table_term), 'band')]
    pallas_call x0 -> x2, Pallas kernels: none -> 136 us  [the longest x1 70.1 us: on_device(): pl.pallas_call(backward_kernel, out_shape=(shape((1440, LANES), BF16), sh...]
    psum x1 -> x0, waiting for transfers between devices: 91.9 us -> none  [on_device(): lax.psum((gain_product, bias_term, table_term), 'band')]
    all_gather x1 -> x0, waiting for transfers between devices: 76.7 us -> none  [on_device(): tile_full = lax.all_gather(tile_portion, 'var', axis=1, tiled=True)]
    unnamed x1 -> x0, blocking collectives: 69 us -> none
    gather x8 -> x0, local copies, waits for them, and re-layouts: 46.5 us -> none  [the longest x1 8.09 us: on_device(): tile_source[outgoing]]
    all_to_all x4 -> x0, waiting for transfers between devices: 44.7 us -> none  [the longest x1 31.2 us: on_device(): lax.all_to_all(info, 'band', split_axis=0, concat_axis=0, tiled=True)]
    reshape x8 -> x1, local copies, waits for them, and re-layouts: 33.5 us -> 0.08 us  [on_device(): three[:, :, 128:].reshape(3, 4, 104)]
  transfers between devices with their start and end apart: 13 -> 0, of which waited for: 5 -> 0; matrix products, arithmetic and copies ran while one was open for 26% -> 0% of each run, Pallas kernels for 0% -> 0%
where the time goes in v1:
time: 149 us; the launch traced here: 148 us
  Pallas kernels  136 us (91%)
  local copies, waits for them, and re-layouts  9.59 us (6%)
  other arithmetic  2.07 us (1%)
    pallas_call x1, Pallas kernels, on_device(): pl.pallas_call(backward_kernel, out_shape=(shape((1440, LANES), BF16), sh...  70.1 us
    pallas_call x1, Pallas kernels, on_device(): pl.pallas_call(forward_kernel, out_shape=(shape((T, LANES), F32), shape((...  65.5 us
    unnamed x10, local copies, waits for them, and re-layouts  9.26 us

profile of v1, /device:TPU:32, one launch (start us, length us, event | category | flops | bytes accessed | tf_op | source)
XLA Modules:
  0.0 148.0 jit_solution(3274899509921082800)
XLA Ops:
  0.6 0.7 sign_compare_fusion.1
  1.3 0.1 ne.99
  1.4 0.7 broadcast_divide_fusion
  2.1 0.1 div.27
  2.2 0.1 rem.55
  2.4 0.1 reshape.171
  2.5 0.6 select_maximum_fusion.places
  3.1 1.9 %copy.15.table = f32[16,45,128]{2,1,0:T(8,128)} copy(f32[16,45,128]{2,0,1:T(8,128)} %param.15) | data formatting | bytes 737280 | tf_op args[5]
  5.0 65.5 %forward.1 = (f32[1536,128]{1,0:T(8,128)}, bf16[1536,128]{1,0:T(8,128)(2,1)}, bf16[640,1536]{1,0:T(8,128)(2,1)}, f32[8,1536]{1,0:T(8,128)}, f32[8,1536]{1,0:T(8,128)}) custom-call(s32[10]{0:T(128)} %ids.1, f32[80]{0:T(128)} %shift.1, f32[80]{0:T(128)} %scale.1, bf16[4,10,16,1440]{3,2,1,0:T(8,128)(2,1)} %fields.1, bf16[640,1024]{1,0:T(8,128)(2,1)} %bitcast.15, ...), custom_call_target="tpu_custom_call" | custom-call | tf_op jit(solution)/shard_map/forward/pallas_call | solution.py:660
  70.4 70.1 %backward.1 = (bf16[1440,128]{1,0:T(8,128)(2,1)}, f32[20,1024]{1,0:T(8,128)}, f32[16,45,128]{2,1,0:T(8,128)}, f32[1,128]{1,0:T(1,128)}, f32[1,128]{1,0:T(1,128)}) custom-call(f32[1536,128]{1,0:T(8,128)} %get-tuple-element.15.pre, bf16[1536,128]{1,0:T(8,128)(2,1)} %get-tuple-element.16.cot, bf16[640,1536]{1,0:T(8,128)(2,1)} %get-tuple-element.17.xb, ...), custom_call_target="tpu_custom_call" | custom-call | tf_op jit(solution)/shard_map/backward/pallas_call | solution.py:687
  140.6 1.9 %copy.16 = f32[16,45,128]{2,0,1:T(8,128)} copy(f32[16,45,128]{2,1,0:T(8,128)} %get-tuple-element.27) | data formatting | bytes 737280
  142.4 1.7 %copy.27 = bf16[1440,128]{1,0:T(8,128)(2,1)} copy(bf16[1440,128]{1,0:T(8,128)(2,1)} %get-tuple-element.40) | data formatting | bytes 737280
  144.2 1.5 %copy.28 = f32[20,1024]{1,0:T(8,128)} copy(f32[20,1024]{1,0:T(8,128)} %get-tuple-element.41) | data formatting | bytes 163840
  145.7 1.1 copy.29
  146.9 1.1 copy.30
  (7 shorter events, 0.0 us)

commit v2 on v0

v2 whole, which is shorter than its diff:
```python
import functools

import jax
import jax.numpy as jnp
from jax import lax
from jax.experimental import pallas as pl
from jax.experimental.pallas import tpu as pltpu
from jax.sharding import PartitionSpec as P

EPS = 1e-05
T = 1536
LANES = 128
NB = 32
NV = 8
PER = 48
USED = 45
E = 1024
PIECE = 384
SENT = 368
F32 = jnp.float32
BF16 = jnp.bfloat16
HI = lax.Precision.HIGHEST


def iota(shape, dim):
    return lax.broadcasted_iota(jnp.int32, shape, dim)


def onehot(cond):
    return jnp.where(cond, 1.0, 0.0).astype(BF16)


def dot(a, b):
    return jnp.dot(a, b, preferred_element_type=F32)


def remote(src, dst, send, recv, v, b):
    return pltpu.make_async_remote_copy(
        src_ref=src,
        dst_ref=dst,
        send_sem=send,
        recv_sem=recv,
        device_id=(v, b),
        device_id_type=pl.DeviceIdType.MESH,
    )


class Place:
    def __init__(self):
        self.v = lax.axis_index("var")
        self.b = lax.axis_index("band")
        self.x = self.v // 2
        self.h = self.v % 2
        self.zl = self.b // 8
        self.y = (self.b // 2) % 4
        self.core = self.b % 2
        self.right = lax.rem(self.x + 1, 4) * 2 + self.h
        self.left = lax.rem(self.x + 3, 4) * 2 + self.h
        self.over = self.x * 2 + 1 - self.h

    def band_peer(self, k):
        return lax.rem(self.b + k, NB)

    def band_source(self, k):
        return lax.rem(self.b + NB - k, NB)


def greet(me, var_peers):
    barrier = pltpu.get_barrier_semaphore()

    @pl.loop(1, NB)
    def _(k):
        pl.semaphore_signal(
            barrier, inc=1, device_id=(me.v, me.band_peer(k)), device_id_type=pl.DeviceIdType.MESH
        )

    for peer in var_peers:
        pl.semaphore_signal(
            barrier, inc=1, device_id=(peer, me.b), device_id_type=pl.DeviceIdType.MESH
        )
    return lambda: pl.semaphore_wait(barrier, NB - 1 + len(var_peers))


def rows(i, n):
    return pl.ds(pl.multiple_of(i * n, n), n)


def exchange_start(me, src, dst, send, recv):
    @pl.loop(1, NB)
    def _(k):
        d = me.band_peer(k)
        remote(src(d), dst(me.b), send.at[d], recv.at[me.b], me.v, d).start()


def exchange_wait_recv(me, src, dst, send, recv):
    @pl.loop(1, NB)
    def _(k):
        s = me.band_source(k)
        remote(src(s), dst(s), send.at[s], recv.at[s], me.v, s).wait_recv()


def exchange_wait_send(me, src, dst, send, recv):
    @pl.loop(1, NB)
    def _(k):
        d = me.band_peer(k)
        remote(src(d), dst(d), send.at[d], recv.at[d], me.v, d).wait_send()


def mix_blocks(me, transposed):
    shape = (LANES, LANES)
    token = iota(shape, 1 if transposed else 0)
    cell = iota(shape, 0 if transposed else 1)
    second = cell >= 64
    j = jnp.where(second, cell - 64, cell)
    first = (me.b + 1) // 2 - 1

    def lat(p):
        u = jnp.clip(
            ((2 * me.b + p).astype(F32) + 0.5) / 4.0 - 0.5, 0.0, 15.0
        )
        w0 = jnp.maximum(1.0 - jnp.abs(u - first.astype(F32)), 0.0)
        w1 = jnp.maximum(1.0 - jnp.abs(u - (first + 1).astype(F32)), 0.0)
        return jnp.where(second, w1, w0)

    def lon(c):
        w = (c.astype(F32) + 0.5) / 4.0 - 0.5
        d = jnp.abs(w - j.astype(F32))
        d = jnp.minimum(d, 45.0 - d)
        return jnp.where(j < 45, jnp.maximum(1.0 - d, 0.0), 0.0)

    lat0, lat1 = lat(0), lat(1)
    low = lon(token)
    end0 = jnp.where(token < 52, lat0 * lon(token + 128), 0.0)
    end1 = jnp.where(
        jnp.logical_and(token >= 52, token < 104), lat1 * lon(token + 76), 0.0
    )
    return [(m).astype(BF16) for m in (lat0 * low, lat1 * low, end0 + end1)]


def nt(a, b):
    return lax.dot_general(a, b, (((1,), (1,)), ((), ())), preferred_element_type=F32)


def sample(s):
    return pl.ds(s * PIECE, PIECE)


def sent(s):
    return pl.ds(s * PIECE, SENT)


def encoder_kernel(
    ids, shift, scale, fields_at, weight_at, table, order, gout, gain_in, bias_in,
    embed, grad_weight, grad_table, grad_gain, grad_bias,
    fields, weight, info, got_info, slotcol, posrow, poscol, slotrow, gpad, cot_out, cot_in, cot,
    xn, sel, sel_end, perm, permb, xt, xb, xrow, wq, part, leg, from_left, from_right,
    zout, zin, window, pre,
    stat, packed, stat_x, packed_z, stat_z, statcol, emb, emb_out, emb_in, dg,
    core_out, core_in, gw, y_out, y_in, zl_out, zl_in,
    outer, outer_in, inner, chip, chip_in, tables,
    load_s, info_s, info_r, cot_s, cot_r, leg_s, leg_r, dir_s, comb_s, left_r, right_r, z_s, z_r,
    sx_s, sx_r, sz_s, sz_r, emb_s, emb_r, dz_s, dz_r, dx_s, dr_r, dl_r, df_s, df_r,
    core_s, core_r, y_s, y_r, zl_s, zl_r, t_s, t_r, tz_s, tz_r, ty_s, ty_r,
):
    me = Place()
    x_peers = [lax.rem(me.x + k, 4) * 2 + me.h for k in range(1, 4)]
    wait_barrier = greet(me, x_peers + [me.over])
    gain = gain_in[...]
    bias = bias_in[...]
    sends = []

    def send(copy):
        copy.start()
        sends.append(copy)

    loads = [pltpu.make_async_copy(weight_at, weight, load_s.at[4])]
    for s in range(4):
        loads.append(pltpu.make_async_copy(fields_at.at[s], fields.at[s], load_s.at[s]))
    for copy in loads:
        copy.start()

    o = order[...].astype(F32)
    pieces = []
    for s in range(4):
        at = 360 * s
        pieces += [o[:, at : at + 128], o[:, at + 180 : at + 308]]
        pieces.append(
            jnp.concatenate(
                [o[:, at + 128 : at + 180], o[:, at + 308 : at + 360],
                 jnp.full((1, 24), 99.0 * 1440.0, F32)], 1
            )
        )
    o = jnp.concatenate(pieces, 1)
    target = jnp.floor((o + 0.5) * (1.0 / 1440.0))
    slot = o - target * 1440.0
    high = jnp.floor(slot * (1.0 / 32.0))
    low = slot - high * 32.0
    to_shard = jnp.where(iota((NB, T), 0).astype(F32) == target, 1.0, 0.0)
    tiles = [to_shard[:, i * 128 : i * 128 + 128] for i in range(12)]
    lane = iota((LANES, LANES), 1)
    above = onehot(iota((LANES, LANES), 0) < lane)
    before = dot(jnp.concatenate(tiles, 0).astype(BF16), above)
    carry = jnp.zeros((NB, 1), F32)
    ranks = []
    for i in range(12):
        ranks.append(
            jnp.sum(tiles[i] * (before[i * NB : i * NB + NB] + carry), 0, keepdims=True)
        )
        carry = carry + jnp.sum(tiles[i], 1, keepdims=True)
    rank = jnp.concatenate(ranks, 1)
    posrow[...] = jnp.broadcast_to(target * PER + rank, (8, T))
    at = iota((LANES, T), 0).astype(F32) == rank
    shards = to_shard.astype(BF16)
    slots = nt(shards, jnp.where(at, high, 0.0).astype(BF16)) * 32.0 + nt(
        shards, jnp.where(at, low, 0.0).astype(BF16)
    )
    slots = jnp.where(iota((NB, LANES), 1) < USED, slots, -1.0)
    for d in range(NB):
        info[d] = jnp.broadcast_to(slots[d : d + 1], (8, LANES))
    wait_barrier()
    info_args = (me, lambda d: info.at[d], lambda s: got_info.at[s], info_s, info_r)
    exchange_start(*info_args)
    got_info[pl.ds(me.b, 1)] = info[pl.ds(me.b, 1)]

    xn[:, :, :, 1408:1536] = jnp.zeros((2, 4, 80, 128), BF16)
    for s in range(4):
        pad = slice(s * PIECE + SENT, (s + 1) * PIECE)
        zero = jnp.zeros((PIECE - SENT, 256), BF16)
        from_left[pad, :] = zero
        from_right[pad, :] = zero
        zin[pad, :] = zero[:, 0:128]
        for c in range(4):
            for hh in range(2):
                dg[c, hh, pad, :] = zero[:, 0:128]

    @pl.loop(0, 8)
    def _(i):
        n = iota((LANES, E), 1)
        k = iota((LANES, E), 0) + i * LANES
        sel[rows(i, LANES), :] = onehot(k == (n & 127) * 8 + (n >> 7))

    @pl.loop(0, 4)
    def _(i):
        n = iota((LANES, E), 1)
        k = iota((LANES, E), 0) + i * LANES
        sel_end[rows(i, LANES), :] = onehot(k == ((n & 127) - 52) * 8 + (n >> 7))

    n = iota((80, 640), 1)
    g = iota((80, 640), 0)
    for dx in range(8):
        perm[dx * 80 : dx * 80 + 80, :] = onehot(n == g * 8 + dx)
    loads[0].wait()
    for i in range(4):
        lanes = slice(i * 256, i * 256 + 256)
        wq[:, lanes] = dot(perm[...], weight[:, lanes]).astype(BF16)
    eye = onehot(iota((PIECE, PIECE), 0) == iota((PIECE, PIECE), 1))

    def patches(ch):
        for s in (2 * ch, 2 * ch + 1):
            loads[1 + s].wait()

            @pl.loop(0, 5)
            def _(pair):
                halves = []
                for j in range(2):
                    k = 2 * pair + j
                    at = ids[k]
                    halves.append((fields[s, k].astype(F32) - shift[at]) * scale[at])
                for p in range(2):
                    both = jnp.concatenate([q[8 * p : 8 * p + 8] for q in halves], 0)
                    xn[p, s, rows(pair, 16), 0:1440] = both.astype(BF16)

        x = [xn[p, 2 * ch : 2 * ch + 2].reshape(160, T) for p in range(2)]
        both = jnp.concatenate(x, 0)
        for i in range(4):
            out = slice(i * 256, i * 256 + 256)
            low = dot(both[:, 0:1024], sel[:, out]).astype(BF16)
            end = (
                dot(x[0][:, 1024:1536], sel[0:512, out])
                + dot(x[1][:, 1024:1536], sel_end[:, out])
            ).astype(BF16)
            for q in range(2):
                at = slice((2 * i + q) * 80, (2 * i + q) * 80 + 80)
                lanes = slice(q * 128, q * 128 + 128)
                for s in range(2):
                    base = (2 * ch + s) * PIECE
                    for p in range(2):
                        first = (2 * p + s) * 80
                        xt[at, base + p * 128 : base + p * 128 + 128] = low[
                            first : first + 80, lanes
                        ]
                    xt[at, base + 256 : base + 384] = end[s * 80 : s * 80 + 80, lanes]

    def partials(s):
        xrow[...] = nt(eye, xt[:, sample(s)]).astype(BF16)
        for j, ahead in ((0, 2), (1, 1), (2, 3), (3, 0)):
            at = lax.rem(me.x + ahead, 4)
            lanes = pl.ds(pl.multiple_of(at * 256, 256), 256)
            part[j, sample(s), :] = dot(xrow[...], wq[:, lanes]).astype(BF16)

    def onward(s):
        return (me.right, me.left) if s % 2 == 0 else (me.left, me.right)

    def start_x(s):
        ahead, back = onward(s)
        send(remote(part.at[0, sent(s)], leg.at[sent(s)], leg_s.at[s], leg_r.at[s], ahead, me.b))
        if s % 2 == 0:
            send(remote(part.at[2, sent(s)], from_right.at[sent(s)], dir_s.at[s], right_r.at[s],
                        back, me.b))
        else:
            send(remote(part.at[1, sent(s)], from_left.at[sent(s)], dir_s.at[s], left_r.at[s],
                        back, me.b))

    def pass_on(s):
        ahead, back = onward(s)
        remote(part.at[0, sent(s)], leg.at[sent(s)], leg_s.at[s], leg_r.at[s],
               back, me.b).wait_recv()
        j = 1 if s % 2 == 0 else 2
        at = sent(s)
        part[j, at, :] = (part[j, at, :].astype(F32) + leg[at, :].astype(F32)).astype(BF16)
        into, sem = (from_left, left_r) if s % 2 == 0 else (from_right, right_r)
        send(remote(part.at[j, at], into.at[at], comb_s.at[s], sem.at[s], ahead, me.b))

    def finish_x(s):
        src = part.at[0, sent(s)]
        remote(src, from_left.at[sent(s)], dir_s.at[s], left_r.at[s], me.left, me.b).wait_recv()
        remote(src, from_right.at[sent(s)], dir_s.at[s], right_r.at[s], me.right, me.b).wait_recv()
        sl = sample(s)
        total = (
            part[3, sl, :].astype(F32) + from_left[sl, :].astype(F32)
        ) + from_right[sl, :].astype(F32)
        mine = jnp.where(me.h == 0, total[:, 0:128], total[:, 128:256])
        other = jnp.where(me.h == 0, total[:, 128:256], total[:, 0:128])
        zout[sl, :] = other.astype(BF16)
        send(remote(zout.at[sent(s)], zin.at[sent(s)], z_s.at[s], z_r.at[s], me.over, me.b))
        pre[sl, :] = mine

    def finish_z(s):
        remote(zout.at[sent(s)], zin.at[sent(s)], z_s.at[s], z_r.at[s], me.over, me.b).wait_recv()
        sl = sample(s)
        pre[sl, :] = pre[sl, :] + zin[sl, :].astype(F32) + jnp.concatenate(position, 0)

    cot_args = (
        me,
        lambda d: cot_out.at[rows(d, PER)],
        lambda s: cot_in.at[rows(s, PER)],
        cot_s,
        cot_r,
    )
    wide = iota((384, T), 1).astype(F32)

    def answer():
        gpad[1440:T, :] = jnp.zeros((T - 1440, LANES), BF16)
        gpad[0:1440, :] = gout[...]
        exchange_wait_recv(*info_args)
        asked = jnp.concatenate([got_info[s][0:1] for s in range(NB)], 0)
        asked = jnp.concatenate([asked, jnp.zeros((LANES - NB, LANES), F32)], 0).T
        for i in range(4):
            at = jnp.concatenate([asked[0:PER, s : s + 1] for s in range(8 * i, 8 * i + 8)], 0)
            slotcol[i * 384 : i * 384 + 384, :] = jnp.broadcast_to(at, (384, LANES))
            cot_out[i * 384 : i * 384 + 384, :] = dot(onehot(at == wide), gpad[...]).astype(BF16)
        exchange_start(*cot_args)
        cot_in[rows(me.b, PER), :] = cot_out[rows(me.b, PER), :]

    def place_cot():
        exchange_wait_recv(*cot_args)
        for i in range(4):
            sl = slice(i * 384, i * 384 + 384)
            cot[sl, :] = dot(onehot(poscol[sl, 0:1] == wide), cot_in[...]).astype(BF16)

    def local_sums(ch):
        lane = iota((PIECE, LANES), 1)
        for j in range(2):
            sl = sample(2 * ch + j)
            a = pre[sl, :]
            g = cot[sl, :].astype(F32) * gain
            block = jnp.zeros((PIECE, LANES), F32)
            for k, q in enumerate((a, a * a, g, g * a)):
                block = jnp.where(lane == 4 * j + k, jnp.sum(q, 1, keepdims=True), block)
            stat[sl, :] = block
        flat = stat[pl.ds(ch * 768, 768), :].T
        packed[ch] = flat[0:8, 0:PIECE] + flat[0:8, PIECE : 2 * PIECE]
        stat_x[ch, pl.ds(me.x, 1)] = packed[ch][None]
        for k in range(1, 4):
            send(remote(packed.at[ch], stat_x.at[ch, me.x], sx_s.at[ch, k - 1],
                        sx_r.at[ch, me.x], x_peers[k - 1], me.b))

    def sums_x(ch):
        for k in range(1, 4):
            src = lax.rem(me.x + 4 - k, 4)
            remote(packed.at[ch], stat_x.at[ch, src], sx_s.at[ch, k - 1], sx_r.at[ch, src],
                   src * 2 + me.h, me.b).wait_recv()
        packed_z[ch] = (stat_x[ch, 0] + stat_x[ch, 1]) + (stat_x[ch, 2] + stat_x[ch, 3])
        send(remote(packed_z.at[ch], stat_z.at[ch], sz_s.at[ch], sz_r.at[ch], me.over, me.b))

    def sums_z(ch):
        remote(packed_z.at[ch], stat_z.at[ch], sz_s.at[ch], sz_r.at[ch], me.over, me.b).wait_recv()
        total = packed_z[ch] + stat_z[ch]
        statcol[ch] = jnp.concatenate([total, jnp.zeros((120, PIECE), F32)], 0).T

    own = dg.at[0, me.h]
    over = dg.at[0, 1 - me.h]
    totals = [jnp.zeros((1, LANES), F32), jnp.zeros((1, LANES), F32)]

    def send_x(block, hh, s):
        k = 1 if s % 2 == 0 else 0
        at = sent(s)
        two = [
            remote(block.at[at], dg.at[1, hh, at], dx_s.at[hh, s, 0], dr_r.at[hh, s],
                   me.right, me.b),
            remote(block.at[at], dg.at[2, hh, at], dx_s.at[hh, s, 1], dl_r.at[hh, s],
                   me.left, me.b),
        ]
        send(two[1 - k])
        send(two[k])

    def norm(ch):
        for j in range(2):
            s = 2 * ch + j
            sl = sample(s)
            s1, s2, sg, sq = [statcol[ch, :, 4 * j + k : 4 * j + k + 1] for k in range(4)]
            mean = s1 / E
            inv = lax.rsqrt(s2 / E - mean * mean + EPS)
            xhat = (pre[sl, :] - mean) * inv
            up = cot[sl, :].astype(F32)
            along = inv * (sq - mean * sg) / E
            d = inv * (up * gain - sg / E - xhat * along)
            own[sl, :] = d.astype(BF16)
            send(remote(own.at[sent(s)], own.at[sent(s)], dz_s.at[s], dz_r.at[s], me.over, me.b))
            send_x(own, me.h, s)
            emb[sl, :] = (xhat * gain + bias).astype(BF16)
            totals[0] = totals[0] + jnp.sum(up * xhat, 0, keepdims=True)
            totals[1] = totals[1] + jnp.sum(up, 0, keepdims=True)

    def over_arrives(s):
        remote(own.at[sent(s)], over.at[sent(s)], dz_s.at[s], dz_r.at[s], me.over, me.b).wait_recv()
        send_x(over, 1 - me.h, s)

    def pass_d(hh, s):
        at = sent(s)
        src = dg.at[0, hh, at]
        if s % 2 == 0:
            remote(src, dg.at[1, hh, at], dx_s.at[hh, s, 0], dr_r.at[hh, s],
                   me.left, me.b).wait_recv()
            send(remote(dg.at[1, hh, at], dg.at[3, hh, at], df_s.at[hh, s], df_r.at[hh, s],
                        me.right, me.b))
        else:
            remote(src, dg.at[2, hh, at], dx_s.at[hh, s, 1], dl_r.at[hh, s],
                   me.right, me.b).wait_recv()
            send(remote(dg.at[2, hh, at], dg.at[3, hh, at], df_s.at[hh, s], df_r.at[hh, s],
                        me.left, me.b))

    def await_d(c):
        for hh in range(2):
            for s in range(4):
                at = sent(s)
                src = dg.at[0, hh, at]
                if c == 1 and s % 2 == 1:
                    remote(src, dg.at[1, hh, at], dx_s.at[hh, s, 0], dr_r.at[hh, s],
                           me.left, me.b).wait_recv()
                if c == 2 and s % 2 == 0:
                    remote(src, dg.at[2, hh, at], dx_s.at[hh, s, 1], dl_r.at[hh, s],
                           me.right, me.b).wait_recv()
                if c == 3:
                    remote(src, dg.at[3, hh, at], df_s.at[hh, s], df_r.at[hh, s],
                           me.left, me.b).wait_recv()

    tall = iota((384, T), 0).astype(F32)
    emb_args = (
        me,
        lambda d: emb_out.at[rows(d, PER)],
        lambda s: emb_in.at[rows(s, PER)],
        emb_s,
        emb_r,
    )

    def pick_emb():
        for i in range(4):
            hot = onehot(posrow[0:1, :] == tall + i * 384.0)
            emb_out[i * 384 : i * 384 + 384, :] = dot(hot, emb[...]).astype(BF16)

    def start_emb():
        exchange_start(*emb_args)
        emb_in[rows(me.b, PER), :] = emb_out[rows(me.b, PER), :]

    def place_emb():
        exchange_wait_recv(*emb_args)
        for i in range(3):
            hot = onehot(slotrow[0:1, :] == iota((480, T), 0).astype(F32) + i * 480.0)
            embed[i * 480 : i * 480 + 480, :] = dot(hot, emb_in[...]).astype(BF16)

    even = me.core == 0
    across = jnp.where(even, lax.rem(me.b + NB - 1, NB), lax.rem(me.b + 1, NB))
    mate = jnp.where(even, me.b + 1, me.b - 1)
    outer_copy = remote(outer, outer_in, t_s.at[0], t_r.at[0], me.v, across)
    chip_copy = remote(chip, chip_in, t_s.at[1], t_r.at[1], me.v, mate)

    def table_rows():
        mixes = mix_blocks(me, True)
        term = jnp.zeros((LANES, LANES), F32)
        for i in range(12):
            term = term + dot(mixes[i % 3], own[i * LANES : (i + 1) * LANES, :])
        outer[...] = jnp.where(even, term[0:48], term[64:112])
        inner[...] = jnp.where(even, term[64:112], term[0:48])
        send(outer_copy)

    def table_chip():
        outer_copy.wait_recv()
        at = iota((48, LANES), 0)
        both = inner[...] + outer_in[...]
        chip[...] = jnp.where(at == 45, totals[0], jnp.where(at == 46, totals[1], both))
        send(chip_copy)

    def table_z():
        chip_copy.wait_recv()
        tables[pl.ds(me.y, 1), pl.ds(me.zl, 1)] = (chip[...] + chip_in[...])[None, None]
        for k in range(1, 4):
            to = lax.rem(me.zl + k, 4)
            here = tables.at[me.y, me.zl]
            send(remote(here, here, tz_s.at[k - 1], tz_r.at[k - 1],
                        me.v, to * 8 + me.y * 2 + me.core))

    def table_y():
        for k in range(1, 4):
            src = lax.rem(me.zl + 4 - k, 4)
            there = tables.at[me.y, src]
            remote(there, there, tz_s.at[k - 1], tz_r.at[k - 1],
                   me.v, src * 8 + me.y * 2 + me.core).wait_recv()
        for k in range(1, 4):
            to = lax.rem(me.y + k, 4)
            here = tables.at[me.y]
            send(remote(here, here, ty_s.at[k - 1], ty_r.at[k - 1],
                        me.v, me.zl * 8 + to * 2 + me.core))

    def table_end():
        for k in range(1, 4):
            src = lax.rem(me.y + 4 - k, 4)
            there = tables.at[src]
            remote(there, there, ty_s.at[k - 1], ty_r.at[k - 1],
                   me.v, me.zl * 8 + src * 2 + me.core).wait_recv()
        gain_total = jnp.zeros((1, LANES), F32)
        bias_total = jnp.zeros((1, LANES), F32)
        for i in range(16):
            block = tables[i % 4, i // 4]
            grad_table[:, i, :] = block[0:45]
            gain_total = gain_total + block[45:46]
            bias_total = bias_total + block[46:47]
        grad_gain[...] = gain_total
        grad_bias[...] = bias_total

    mate_core = 1 - me.core

    def multiply(c):
        right = jnp.concatenate([dg[c, 0], dg[c, 1]], 1)
        theirs = xb[pl.ds(pl.multiple_of(mate_core * 320, 320), 320), :]
        core_out[c] = dot(theirs, right).astype(BF16)
        send(remote(core_out.at[c], core_in.at[c], core_s.at[c], core_r.at[c], me.v, mate))
        mine = xb[pl.ds(pl.multiple_of(me.core * 320, 320), 320), :]
        gw[c] = dot(mine, right)

    def over_y(c):
        remote(core_out.at[c], core_in.at[c], core_s.at[c], core_r.at[c], me.v, mate).wait_recv()
        y_out[c] = (gw[c] + core_in[c].astype(F32)).astype(BF16)
        for k in range(1, 4):
            to = lax.rem(me.y + k, 4)
            src = y_out.at[c, rows(to, 80)]
            send(remote(src, y_in.at[c, k - 1], y_s.at[c, k - 1], y_r.at[c, k - 1],
                        me.v, me.zl * 8 + to * 2 + me.core))

    spread_r = iota((128, 80), 0)
    spread_c = iota((128, 80), 1)
    inside = spread_r & 31
    spread = onehot(
        jnp.logical_and(inside < 20, spread_c == (spread_r >> 5) * 20 + inside)
    )

    def over_z(c):
        total = y_out[c, rows(me.y, 80), :].astype(F32)
        for k in range(1, 4):
            src = lax.rem(me.y + 4 - k, 4)
            remote(y_out.at[c, rows(src, 80)], y_in.at[c, k - 1], y_s.at[c, k - 1],
                   y_r.at[c, k - 1], me.v, me.zl * 8 + src * 2 + me.core).wait_recv()
            total = total + y_in[c, k - 1].astype(F32)
        zl_out[c] = dot(spread, total.astype(BF16)).astype(BF16)
        for k in range(1, 4):
            to = lax.rem(me.zl + k, 4)
            send(remote(zl_out.at[c, rows(to, 32)], zl_in.at[c, k - 1], zl_s.at[c, k - 1],
                        zl_r.at[c, k - 1], me.v, to * 8 + me.y * 2 + me.core))

    def finish(c):
        total = zl_out[c, rows(me.zl, 32), :].astype(F32)
        for k in range(1, 4):
            src = lax.rem(me.zl + 4 - k, 4)
            remote(zl_out.at[c, rows(src, 32)], zl_in.at[c, k - 1], zl_s.at[c, k - 1],
                   zl_r.at[c, k - 1], me.v, src * 8 + me.y * 2 + me.core).wait_recv()
            total = total + zl_in[c, k - 1].astype(F32)
        x = lax.rem(me.x + (0, 3, 1, 2)[c], 4)
        grad_weight[:, pl.ds(pl.multiple_of(x * 256, 256), 256)] = total[0:20]

    patches(0)
    partials(0)
    start_x(0)
    partials(1)
    start_x(1)
    answer()
    patches(1)
    pass_on(0)
    pass_on(1)
    partials(2)
    start_x(2)
    partials(3)
    start_x(3)

    first = (me.b + 1) // 2 - 1
    window[...] = jnp.zeros((LANES, LANES), F32)
    level = iota((45, 16, LANES), 1)
    all_rows = table[...]
    window[0:45, :] = jnp.sum(jnp.where(level == first, all_rows, 0.0), 1)
    window[64:109, :] = jnp.sum(jnp.where(level == first + 1, all_rows, 0.0), 1)
    position = [
        jnp.dot(m.astype(F32), window[...], precision=HI, preferred_element_type=F32)
        for m in mix_blocks(me, False)
    ]
    poscol[...] = jnp.concatenate([posrow[...], jnp.zeros((120, T), F32)], 0).T

    finish_x(0)
    finish_x(1)

    r = iota((640, 1), 0)

    def steps(a, size, count):
        at = jnp.zeros_like(a)
        for i in range(1, count):
            at = at + jnp.where(a >= i * size, 1, 0)
        return at

    core = steps(r, 320, 2)
    r = r - 320 * core
    y = steps(r, 80, 4)
    r = r - 80 * y
    zl = steps(r, 20, 4)
    n = 20 * (zl * 8 + y * 2 + core) + r - 20 * zl
    permb[...] = onehot(iota((640, 640), 1) == (n & 7) * 80 + (n >> 3))

    @pl.loop(0, 6)
    def _(i):
        xb[:, rows(i, 256)] = dot(permb[...], xt[:, rows(i, 256)]).astype(BF16)

    pass_on(2)
    pass_on(3)
    place_cot()
    for i in range(12):
        sl = slice(i * LANES, (i + 1) * LANES)
        slotrow[:, sl] = slotcol[sl, :].T[0:8]
    finish_z(0)
    finish_z(1)
    local_sums(0)
    finish_x(2)
    finish_x(3)
    sums_x(0)
    sums_z(0)
    norm(0)
    finish_z(2)
    finish_z(3)
    local_sums(1)
    over_arrives(0)
    over_arrives(1)
    sums_x(1)
    pass_d(me.h, 0)
    pass_d(me.h, 1)
    sums_z(1)
    norm(1)
    pass_d(1 - me.h, 0)
    pass_d(1 - me.h, 1)
    pick_emb()
    table_rows()
    over_arrives(2)
    over_arrives(3)
    start_emb()
    pass_d(me.h, 2)
    pass_d(me.h, 3)
    multiply(0)
    table_chip()
    over_y(0)
    table_z()
    pass_d(1 - me.h, 2)
    pass_d(1 - me.h, 3)
    await_d(1)
    multiply(1)
    over_z(0)
    over_y(1)
    table_y()
    await_d(2)
    multiply(2)
    over_z(1)
    over_y(2)
    place_emb()
    finish(0)
    over_z(2)
    await_d(3)
    multiply(3)
    finish(1)
    over_y(3)
    finish(2)
    table_end()
    over_z(3)
    finish(3)
    for copy in sends:
        copy.wait_send()
    exchange_wait_send(*info_args)
    exchange_wait_send(*cot_args)
    exchange_wait_send(*emb_args)


def result_kernel(*refs):
    count = len(refs) // 2
    for i in range(count):
        refs[count + i][...] = refs[i][...]


def dma(*shape):
    return pltpu.SemaphoreType.DMA(shape)


def vmem(shape, dtype=BF16):
    return pltpu.VMEM(shape, dtype)


def on_device(
    fields, var_ids, var_shift, var_scale, patch_weight, pos_table,
    layer_norm_gain, layer_norm_bias, order, grad_out,
):
    here = pl.BlockSpec(memory_space=pltpu.VMEM)
    scalars = pl.BlockSpec(memory_space=pltpu.SMEM)
    anywhere = pl.BlockSpec(memory_space=pl.ANY)
    shape = jax.ShapeDtypeStruct
    out_shape = (
        shape((1440, LANES), BF16),
        shape((20, E), F32),
        shape((45, 16, LANES), F32),
        shape((1, LANES), F32),
        shape((1, LANES), F32),
    )
    results = pl.pallas_call(
        encoder_kernel,
        out_shape=out_shape,
        in_specs=[scalars] * 3 + [anywhere] * 2 + [here] * 5,
        out_specs=(here,) * 5,
        scratch_shapes=[
            vmem((4, 10, 16, 1440)), vmem((640, E)),
            vmem((NB, 8, LANES), F32), vmem((NB, 8, LANES), F32), vmem((T, LANES), F32),
            vmem((8, T), F32), vmem((T, LANES), F32), vmem((8, T), F32),
            vmem((T, LANES)), vmem((T, LANES)), vmem((T, LANES)), vmem((T, LANES)),
            vmem((2, 4, 80, T)), vmem((E, E)), vmem((512, E)),
            vmem((640, 640)), vmem((640, 640)), vmem((640, T)), vmem((640, T)),
            vmem((PIECE, 640)), vmem((640, E)),
            vmem((4, T, 256)), vmem((T, 256)), vmem((T, 256)), vmem((T, 256)),
            vmem((T, LANES)), vmem((T, LANES)), vmem((LANES, LANES), F32), vmem((T, LANES), F32),
            vmem((T, LANES), F32), vmem((2, 8, PIECE), F32), vmem((2, 4, 8, PIECE), F32),
            vmem((2, 8, PIECE), F32), vmem((2, 8, PIECE), F32), vmem((2, PIECE, LANES), F32),
            vmem((T, LANES)), vmem((T, LANES)), vmem((T, LANES)), vmem((4, 2, T, LANES)),
            vmem((4, 320, 256)), vmem((4, 320, 256)), vmem((4, 320, 256), F32),
            vmem((4, 320, 256)), vmem((4, 3, 80, 256)),
            vmem((4, 128, 256)), vmem((4, 3, 32, 256)),
            vmem((48, LANES), F32), vmem((48, LANES), F32), vmem((48, LANES), F32),
            vmem((48, LANES), F32), vmem((48, LANES), F32), vmem((4, 4, 48, LANES), F32),
            dma(5), dma(NB), dma(NB), dma(NB), dma(NB),
            dma(4), dma(4), dma(4), dma(4), dma(4), dma(4), dma(4), dma(4),
            dma(2, 3), dma(2, 4), dma(2), dma(2), dma(NB), dma(NB), dma(4), dma(4),
            dma(2, 4, 2), dma(2, 4), dma(2, 4), dma(2, 4), dma(2, 4),
            dma(4), dma(4), dma(4, 3), dma(4, 3), dma(4, 3), dma(4, 3),
            dma(2), dma(2), dma(3), dma(3), dma(3), dma(3),
        ],
        compiler_params=pltpu.CompilerParams(
            has_side_effects=True, vmem_limit_bytes=58 * 1024 * 1024, collective_id=0
        ),
        name="encoder",
    )(
        var_ids, var_shift, var_scale, fields, patch_weight.reshape(640, E),
        pos_table.transpose(1, 0, 2), order.reshape(1, 1440), grad_out,
        layer_norm_gain.reshape(1, LANES), layer_norm_bias.reshape(1, LANES),
    )
    embed, grad_weight, grad_table, grad_gain, grad_bias = pl.pallas_call(
        result_kernel,
        out_shape=out_shape,
        in_specs=[here] * 5,
        out_specs=(here,) * 5,
        name="results",
    )(*results)
    return (
        embed, grad_weight, grad_table.transpose(1, 0, 2),
        grad_gain.reshape(LANES), grad_bias.reshape(LANES),
    )


def solution(mesh):
    in_specs = (
        P(None, "var", "band", None),
        P("var"),
        P(),
        P(),
        P("var", None, None),
        P(None, None, "var"),
        P("var"),
        P("var"),
        P("band"),
        P("band", "var"),
    )
    out_specs = (
        P("band", "var"),
        P(("var", "band"), None),
        P(None, None, "var"),
        P("var"),
        P("var"),
    )
    return jax.shard_map(
        on_device, mesh=mesh, in_specs=in_specs, out_specs=out_specs, check_vma=False
    )
```

time: 703 us -> 119 us (0.17); the launches traced: 692 us -> 117 us
  blocking collectives: 224 us -> 0 us
  waiting for transfers between devices: 213 us -> 0 us
  local copies, waits for them, and re-layouts: 149 us -> 1.29 us
  Pallas kernels: 0 us -> 115 us
  starting transfers between devices: 49.3 us -> 0 us
  other arithmetic: 25.8 us -> 0 us
  matrix products: 15.9 us -> 0 us
  between operations: 15.1 us -> 0.64 us
    psum x3 -> x0, blocking collectives: 155 us -> none  [the longest x1 58 us: on_device(): lax.psum((gain_product, bias_term, table_term), 'band')]
    pallas_call x0 -> x2, Pallas kernels: none -> 115 us  [the longest x1 113 us: on_device(): pl.pallas_call(encoder_kernel, out_shape=out_shape, in_specs=[scalars] *...]
    psum x1 -> x0, waiting for transfers between devices: 91.9 us -> none  [on_device(): lax.psum((gain_product, bias_term, table_term), 'band')]
    all_gather x1 -> x0, waiting for transfers between devices: 76.7 us -> none  [on_device(): tile_full = lax.all_gather(tile_portion, 'var', axis=1, tiled=True)]
    unnamed x1 -> x0, blocking collectives: 69 us -> none
    gather x8 -> x0, local copies, waits for them, and re-layouts: 46.5 us -> none  [the longest x1 8.09 us: on_device(): tile_source[outgoing]]
    all_to_all x4 -> x0, waiting for transfers between devices: 44.7 us -> none  [the longest x1 31.2 us: on_device(): lax.all_to_all(info, 'band', split_axis=0, concat_axis=0, tiled=True)]
    reshape x8 -> x1, local copies, waits for them, and re-layouts: 33.5 us -> 1.29 us  [on_device(): order.reshape(1, 1440)]
  transfers between devices with their start and end apart: 13 -> 0, of which waited for: 5 -> 0; matrix products, arithmetic and copies ran while one was open for 26% -> 0% of each run, Pallas kernels for 0% -> 0%
where the time goes in v2:
time: 119 us; the launch traced here: 117 us
  Pallas kernels  115 us (97%)
  local copies, waits for them, and re-layouts  1.29 us (1%)
    pallas_call x1, Pallas kernels, on_device(): pl.pallas_call(encoder_kernel, out_shape=out_shape, in_specs=[scalars] *...  113 us

profile of v2, /device:TPU:32, one launch (start us, length us, event | category | flops | bytes accessed | tf_op | source)
XLA Modules:
  0.0 117.1 jit_solution(241056319811036690)
XLA Ops:
  0.6 1.3 %reshape.29.order = s32[1,1440]{1,0:T(1,128)} reshape(s32[1440]{0:T(1024)} %param.18) | data formatting | bytes 11520 | tf_op jit(solution)/shard_map/reshape | solution.py:780
  1.9 113.1 %encoder.1 = (bf16[1440,128]{1,0:T(8,128)(2,1)}, f32[20,1024]{1,0:T(8,128)}, f32[45,16,128]{2,1,0:T(8,128)}, f32[1,128]{1,0:T(1,128)}, f32[1,128]{1,0:T(1,128)}) custom-call(s32[10]{0:T(128)} %ids.1, f32[80]{0:T(128)} %shift.1, f32[80]{0:T(128)} %scale.1, bf16[4,10,16,1440]{3,2,1,0:T(8,128)(2,1)} %fields_at.1, bf16[640,1024]{1,0:T(8,128)(2,1)} %bitcast.7, ...), custom_call_target="tpu_custom_call" | custom-call | tf_op jit(solution)/shard_map/encoder/pallas_call | solution.py:744
  115.0 2.1 %results.1 = (bf16[1440,128]{1,0:T(8,128)(2,1)}, f32[20,1024]{1,0:T(8,128)}, f32[45,16,128]{2,1,0:T(8,128)}, f32[1,128]{1,0:T(1,128)}, f32[1,128]{1,0:T(1,128)}) custom-call(bf16[1440,128]{1,0:T(8,128)(2,1)} %get-tuple-element.15.refs_0_, f32[20,1024]{1,0:T(8,128)} %get-tuple-element.16.refs_1_, f32[45,16,128]{2,1,0:T(8,128)} %get-tuple-element.17.refs_2_, ...), custom_call_target="tpu_custom_call" | custom-call | tf_op jit(solution)/shard_map/results/pallas_call | solution.py:783

commit v3 on v2

--- a/solution.py
+++ b/solution.py
@@ -149,22 +149,25 @@
     return pl.ds(s * PIECE, SENT)
 
 
+def half(s, f):
+    return pl.ds(s * PIECE + 192 * f, 192 - 16 * f)
+
+
 def encoder_kernel(
     ids, shift, scale, fields_at, weight_at, table, order, gout, gain_in, bias_in,
     embed, grad_weight, grad_table, grad_gain, grad_bias,
     fields, weight, info, got_info, slotcol, posrow, poscol, slotrow, gpad, cot_out, cot_in, cot,
     xn, sel, sel_end, perm, permb, xt, xb, xrow, wq, part, leg, from_left, from_right,
     zout, zin, window, pre,
-    stat, packed, stat_x, packed_z, stat_z, statcol, emb, emb_out, emb_in, dg,
-    core_out, core_in, gw, y_out, y_in, zl_out, zl_in,
+    packed, sums_in, emb, emb_out, emb_in, dg,
+    first, core_out, core_in, gw, y_out, y_in, zl_out, zl_in,
     outer, outer_in, inner, chip, chip_in, tables,
     load_s, info_s, info_r, cot_s, cot_r, leg_s, leg_r, dir_s, comb_s, left_r, right_r, z_s, z_r,
-    sx_s, sx_r, sz_s, sz_r, emb_s, emb_r, dz_s, dz_r, dx_s, dr_r, dl_r, df_s, df_r,
+    sum_s, sum_r, emb_s, emb_r, dz_s, dz_r, dx_s, dr_r, dl_r, df_s, df_r,
     core_s, core_r, y_s, y_r, zl_s, zl_r, t_s, t_r, tz_s, tz_r, ty_s, ty_r,
 ):
     me = Place()
-    x_peers = [lax.rem(me.x + k, 4) * 2 + me.h for k in range(1, 4)]
-    wait_barrier = greet(me, x_peers + [me.over])
+    wait_barrier = greet(me, [lax.rem(me.v + k, NV) for k in range(1, NV)])
     gain = gain_in[...]
     bias = bias_in[...]
     sends = []
@@ -179,48 +182,49 @@
     for copy in loads:
         copy.start()
 
-    o = order[...].astype(F32)
-    pieces = []
-    for s in range(4):
-        at = 360 * s
-        pieces += [o[:, at : at + 128], o[:, at + 180 : at + 308]]
-        pieces.append(
-            jnp.concatenate(
-                [o[:, at + 128 : at + 180], o[:, at + 308 : at + 360],
-                 jnp.full((1, 24), 99.0 * 1440.0, F32)], 1
+    info_args = (me, lambda d: info.at[d], lambda s: got_info.at[s], info_s, info_r)
+
+    def ask():
+        o = order[...].reshape(1, 1440).astype(F32)
+        pieces = []
+        for s in range(4):
+            at = 360 * s
+            pieces += [o[:, at : at + 128], o[:, at + 180 : at + 308]]
+            pieces.append(
+                jnp.concatenate(
+                    [o[:, at + 128 : at + 180], o[:, at + 308 : at + 360],
+                     jnp.full((1, 24), 99.0 * 1440.0, F32)], 1
+                )
             )
+        o = jnp.concatenate(pieces, 1)
+        target = jnp.floor((o + 0.5) * (1.0 / 1440.0))
+        slot = o - target * 1440.0
+        high = jnp.floor(slot * (1.0 / 32.0))
+        low = slot - high * 32.0
+        to_shard = jnp.where(iota((NB, T), 0).astype(F32) == target, 1.0, 0.0)
+        tiles = [to_shard[:, i * 128 : i * 128 + 128] for i in range(12)]
+        above = onehot(iota((LANES, LANES), 0) < iota((LANES, LANES), 1))
+        before = dot(jnp.concatenate(tiles, 0).astype(BF16), above)
+        carry = jnp.zeros((NB, 1), F32)
+        ranks = []
+        for i in range(12):
+            ranks.append(
+                jnp.sum(tiles[i] * (before[i * NB : i * NB + NB] + carry), 0, keepdims=True)
+            )
+            carry = carry + jnp.sum(tiles[i], 1, keepdims=True)
+        rank = jnp.concatenate(ranks, 1)
+        posrow[...] = jnp.broadcast_to(target * PER + rank, (8, T))
+        at = iota((LANES, T), 0).astype(F32) == rank
+        shards = to_shard.astype(BF16)
+        slots = nt(shards, jnp.where(at, high, 0.0).astype(BF16)) * 32.0 + nt(
+            shards, jnp.where(at, low, 0.0).astype(BF16)
         )
-    o = jnp.concatenate(pieces, 1)
-    target = jnp.floor((o + 0.5) * (1.0 / 1440.0))
-    slot = o - target * 1440.0
-    high = jnp.floor(slot * (1.0 / 32.0))
-    low = slot - high * 32.0
-    to_shard = jnp.where(iota((NB, T), 0).astype(F32) == target, 1.0, 0.0)
-    tiles = [to_shard[:, i * 128 : i * 128 + 128] for i in range(12)]
-    lane = iota((LANES, LANES), 1)
-    above = onehot(iota((LANES, LANES), 0) < lane)
-    before = dot(jnp.concatenate(tiles, 0).astype(BF16), above)
-    carry = jnp.zeros((NB, 1), F32)
-    ranks = []
-    for i in range(12):
-        ranks.append(
-            jnp.sum(tiles[i] * (before[i * NB : i * NB + NB] + carry), 0, keepdims=True)
-        )
-        carry = carry + jnp.sum(tiles[i], 1, keepdims=True)
-    rank = jnp.concatenate(ranks, 1)
-    posrow[...] = jnp.broadcast_to(target * PER + rank, (8, T))
-    at = iota((LANES, T), 0).astype(F32) == rank
-    shards = to_shard.astype(BF16)
-    slots = nt(shards, jnp.where(at, high, 0.0).astype(BF16)) * 32.0 + nt(
-        shards, jnp.where(at, low, 0.0).astype(BF16)
-    )
-    slots = jnp.where(iota((NB, LANES), 1) < USED, slots, -1.0)
-    for d in range(NB):
-        info[d] = jnp.broadcast_to(slots[d : d + 1], (8, LANES))
-    wait_barrier()
-    info_args = (me, lambda d: info.at[d], lambda s: got_info.at[s], info_s, info_r)
-    exchange_start(*info_args)
-    got_info[pl.ds(me.b, 1)] = info[pl.ds(me.b, 1)]
+        slots = jnp.where(iota((NB, LANES), 1) < USED, slots, -1.0)
+        for d in range(NB):
+            info[d] = jnp.broadcast_to(slots[d : d + 1], (8, LANES))
+        wait_barrier()
+        exchange_start(*info_args)
+        got_info[pl.ds(me.b, 1)] = info[pl.ds(me.b, 1)]
 
     xn[:, :, :, 1408:1536] = jnp.zeros((2, 4, 80, 128), BF16)
     for s in range(4):
@@ -298,33 +302,34 @@
             lanes = pl.ds(pl.multiple_of(at * 256, 256), 256)
             part[j, sample(s), :] = dot(xrow[...], wq[:, lanes]).astype(BF16)
 
-    def onward(s):
-        return (me.right, me.left) if s % 2 == 0 else (me.left, me.right)
-
     def start_x(s):
-        ahead, back = onward(s)
-        send(remote(part.at[0, sent(s)], leg.at[sent(s)], leg_s.at[s], leg_r.at[s], ahead, me.b))
-        if s % 2 == 0:
-            send(remote(part.at[2, sent(s)], from_right.at[sent(s)], dir_s.at[s], right_r.at[s],
-                        back, me.b))
-        else:
-            send(remote(part.at[1, sent(s)], from_left.at[sent(s)], dir_s.at[s], left_r.at[s],
-                        back, me.b))
+        for f in range(2):
+            ahead, back = (me.right, me.left) if f == 0 else (me.left, me.right)
+            at = half(s, f)
+            send(remote(part.at[0, at], leg.at[at], leg_s.at[s, f], leg_r.at[s, f], ahead, me.b))
+            src, into, sem = (part.at[2], from_right, right_r) if f == 0 else (
+                part.at[1], from_left, left_r)
+            send(remote(src.at[at], into.at[at], dir_s.at[s, f], sem.at[s, f], back, me.b))
 
     def pass_on(s):
-        ahead, back = onward(s)
-        remote(part.at[0, sent(s)], leg.at[sent(s)], leg_s.at[s], leg_r.at[s],
-               back, me.b).wait_recv()
-        j = 1 if s % 2 == 0 else 2
-        at = sent(s)
-        part[j, at, :] = (part[j, at, :].astype(F32) + leg[at, :].astype(F32)).astype(BF16)
-        into, sem = (from_left, left_r) if s % 2 == 0 else (from_right, right_r)
-        send(remote(part.at[j, at], into.at[at], comb_s.at[s], sem.at[s], ahead, me.b))
+        for f in range(2):
+            ahead, back = (me.right, me.left) if f == 0 else (me.left, me.right)
+            at = half(s, f)
+            remote(part.at[0, at], leg.at[at], leg_s.at[s, f], leg_r.at[s, f],
+                   back, me.b).wait_recv()
+            j = 1 + f
+            part[j, at, :] = (part[j, at, :].astype(F32) + leg[at, :].astype(F32)).astype(BF16)
+            into, sem = (from_left, left_r) if f == 0 else (from_right, right_r)
+            send(remote(part.at[j, at], into.at[at], comb_s.at[s, f], sem.at[s, f], ahead, me.b))
 
     def finish_x(s):
-        src = part.at[0, sent(s)]
-        remote(src, from_left.at[sent(s)], dir_s.at[s], left_r.at[s], me.left, me.b).wait_recv()
-        remote(src, from_right.at[sent(s)], dir_s.at[s], right_r.at[s], me.right, me.b).wait_recv()
+        for f in range(2):
+            at = half(s, f)
+            src = part.at[0, at]
+            remote(src, from_left.at[at], dir_s.at[s, f], left_r.at[s, f],
+                   me.left, me.b).wait_recv()
+            remote(src, from_right.at[at], dir_s.at[s, f], right_r.at[s, f],
+                   me.right, me.b).wait_recv()
         sl = sample(s)
         total = (
             part[3, sl, :].astype(F32) + from_left[sl, :].astype(F32)
@@ -368,69 +373,62 @@
             sl = slice(i * 384, i * 384 + 384)
             cot[sl, :] = dot(onehot(poscol[sl, 0:1] == wide), cot_in[...]).astype(BF16)
 
-    def local_sums(ch):
+    def local_sums(s):
+        sl = sample(s)
         lane = iota((PIECE, LANES), 1)
-        for j in range(2):
-            sl = sample(2 * ch + j)
-            a = pre[sl, :]
-            g = cot[sl, :].astype(F32) * gain
-            block = jnp.zeros((PIECE, LANES), F32)
-            for k, q in enumerate((a, a * a, g, g * a)):
-                block = jnp.where(lane == 4 * j + k, jnp.sum(q, 1, keepdims=True), block)
-            stat[sl, :] = block
-        flat = stat[pl.ds(ch * 768, 768), :].T
-        packed[ch] = flat[0:8, 0:PIECE] + flat[0:8, PIECE : 2 * PIECE]
-        stat_x[ch, pl.ds(me.x, 1)] = packed[ch][None]
-        for k in range(1, 4):
-            send(remote(packed.at[ch], stat_x.at[ch, me.x], sx_s.at[ch, k - 1],
-                        sx_r.at[ch, me.x], x_peers[k - 1], me.b))
-
-    def sums_x(ch):
-        for k in range(1, 4):
-            src = lax.rem(me.x + 4 - k, 4)
-            remote(packed.at[ch], stat_x.at[ch, src], sx_s.at[ch, k - 1], sx_r.at[ch, src],
-                   src * 2 + me.h, me.b).wait_recv()
-        packed_z[ch] = (stat_x[ch, 0] + stat_x[ch, 1]) + (stat_x[ch, 2] + stat_x[ch, 3])
-        send(remote(packed_z.at[ch], stat_z.at[ch], sz_s.at[ch], sz_r.at[ch], me.over, me.b))
-
-    def sums_z(ch):
-        remote(packed_z.at[ch], stat_z.at[ch], sz_s.at[ch], sz_r.at[ch], me.over, me.b).wait_recv()
-        total = packed_z[ch] + stat_z[ch]
-        statcol[ch] = jnp.concatenate([total, jnp.zeros((120, PIECE), F32)], 0).T
+        lane = jnp.where(iota((PIECE, LANES), 0) < 256, lane, lane - 4)
+        a = pre[sl, :]
+        g = cot[sl, :].astype(F32) * gain
+        block = jnp.zeros((PIECE, LANES), F32)
+        for k, q in enumerate((a, a * a, g, g * a)):
+            block = jnp.where(lane == k, jnp.sum(q, 1, keepdims=True), block)
+        flat = block.T[0:8]
+        packed[s, :, 0:128] = flat[:, 0:128] + flat[:, 256:384]
+        packed[s, :, 128:256] = flat[:, 128:256]
+        sums_in[s, pl.ds(me.v, 1)] = packed[s][None]
+        for k in range(1, NV):
+            send(remote(packed.at[s], sums_in.at[s, me.v], sum_s.at[s, k - 1],
+                        sum_r.at[s, me.v], lax.rem(me.v + k, NV), me.b))
+
+    def all_sums(s):
+        for k in range(1, NV):
+            src = lax.rem(me.v + NV - k, NV)
+            remote(packed.at[s], sums_in.at[s, src], sum_s.at[s, k - 1], sum_r.at[s, src],
+                   src, me.b).wait_recv()
+        total = sums_in[s, 0]
+        for k in range(1, NV):
+            total = total + sums_in[s, k]
+        return jnp.concatenate([total, jnp.zeros((120, 256), F32)], 0).T
 
     own = dg.at[0, me.h]
     over = dg.at[0, 1 - me.h]
     totals = [jnp.zeros((1, LANES), F32), jnp.zeros((1, LANES), F32)]
 
     def send_x(block, hh, s):
-        k = 1 if s % 2 == 0 else 0
         at = sent(s)
-        two = [
-            remote(block.at[at], dg.at[1, hh, at], dx_s.at[hh, s, 0], dr_r.at[hh, s],
-                   me.right, me.b),
-            remote(block.at[at], dg.at[2, hh, at], dx_s.at[hh, s, 1], dl_r.at[hh, s],
-                   me.left, me.b),
+        send(remote(block.at[at], dg.at[1, hh, at], dx_s.at[hh, s, 0], dr_r.at[hh, s],
+                    me.right, me.b))
+        send(remote(block.at[at], dg.at[2, hh, at], dx_s.at[hh, s, 1], dl_r.at[hh, s],
+                    me.left, me.b))
+
+    def norm(s):
+        col = all_sums(s)
+        sl = sample(s)
+        s1, s2, sg, sq = [
+            jnp.concatenate([col[:, k : k + 1], col[0:128, 4 + k : 5 + k]], 0) for k in range(4)
         ]
-        send(two[1 - k])
-        send(two[k])
-
-    def norm(ch):
-        for j in range(2):
-            s = 2 * ch + j
-            sl = sample(s)
-            s1, s2, sg, sq = [statcol[ch, :, 4 * j + k : 4 * j + k + 1] for k in range(4)]
-            mean = s1 / E
-            inv = lax.rsqrt(s2 / E - mean * mean + EPS)
-            xhat = (pre[sl, :] - mean) * inv
-            up = cot[sl, :].astype(F32)
-            along = inv * (sq - mean * sg) / E
-            d = inv * (up * gain - sg / E - xhat * along)
-            own[sl, :] = d.astype(BF16)
-            send(remote(own.at[sent(s)], own.at[sent(s)], dz_s.at[s], dz_r.at[s], me.over, me.b))
-            send_x(own, me.h, s)
-            emb[sl, :] = (xhat * gain + bias).astype(BF16)
-            totals[0] = totals[0] + jnp.sum(up * xhat, 0, keepdims=True)
-            totals[1] = totals[1] + jnp.sum(up, 0, keepdims=True)
+        mean = s1 / E
+        inv = lax.rsqrt(s2 / E - mean * mean + EPS)
+        xhat = (pre[sl, :] - mean) * inv
+        up = cot[sl, :].astype(F32)
+        along = inv * (sq - mean * sg) / E
+        d = inv * (up * gain - sg / E - xhat * along)
+        own[sl, :] = d.astype(BF16)
+        send(remote(own.at[sent(s)], own.at[sent(s)], dz_s.at[s], dz_r.at[s], me.over, me.b))
+        send_x(own, me.h, s)
+        emb[sl, :] = (xhat * gain + bias).astype(BF16)
+        totals[0] = totals[0] + jnp.sum(up * xhat, 0, keepdims=True)
+        totals[1] = totals[1] + jnp.sum(up, 0, keepdims=True)
 
     def over_arrives(s):
         remote(own.at[sent(s)], over.at[sent(s)], dz_s.at[s], dz_r.at[s], me.over, me.b).wait_recv()
@@ -439,31 +437,23 @@
     def pass_d(hh, s):
         at = sent(s)
         src = dg.at[0, hh, at]
-        if s % 2 == 0:
-            remote(src, dg.at[1, hh, at], dx_s.at[hh, s, 0], dr_r.at[hh, s],
-                   me.left, me.b).wait_recv()
-            send(remote(dg.at[1, hh, at], dg.at[3, hh, at], df_s.at[hh, s], df_r.at[hh, s],
-                        me.right, me.b))
-        else:
-            remote(src, dg.at[2, hh, at], dx_s.at[hh, s, 1], dl_r.at[hh, s],
-                   me.right, me.b).wait_recv()
-            send(remote(dg.at[2, hh, at], dg.at[3, hh, at], df_s.at[hh, s], df_r.at[hh, s],
-                        me.left, me.b))
-
-    def await_d(c):
-        for hh in range(2):
-            for s in range(4):
-                at = sent(s)
-                src = dg.at[0, hh, at]
-                if c == 1 and s % 2 == 1:
-                    remote(src, dg.at[1, hh, at], dx_s.at[hh, s, 0], dr_r.at[hh, s],
-                           me.left, me.b).wait_recv()
-                if c == 2 and s % 2 == 0:
-                    remote(src, dg.at[2, hh, at], dx_s.at[hh, s, 1], dl_r.at[hh, s],
-                           me.right, me.b).wait_recv()
-                if c == 3:
-                    remote(src, dg.at[3, hh, at], df_s.at[hh, s], df_r.at[hh, s],
-                           me.left, me.b).wait_recv()
+        remote(src, dg.at[1, hh, at], dx_s.at[hh, s, 0], dr_r.at[hh, s], me.left, me.b).wait_recv()
+        at = half(s, 0)
+        send(remote(dg.at[1, hh, at], dg.at[3, hh, at], df_s.at[hh, s, 0], df_r.at[hh, s, 0],
+                    me.right, me.b))
+        at = sent(s)
+        remote(src, dg.at[2, hh, at], dx_s.at[hh, s, 1], dl_r.at[hh, s], me.right, me.b).wait_recv()
+        at = half(s, 1)
+        send(remote(dg.at[2, hh, at], dg.at[3, hh, at], df_s.at[hh, s, 1], df_r.at[hh, s, 1],
+                    me.left, me.b))
+
+    def await_d(samples):
+        for s in samples:
+            for hh in range(2):
+                for f in range(2):
+                    at = half(s, f)
+                    remote(dg.at[0, hh, at], dg.at[3, hh, at], df_s.at[hh, s, f],
+                           df_r.at[hh, s, f], me.left, me.b).wait_recv()
 
     tall = iota((384, T), 0).astype(F32)
     emb_args = (
@@ -550,13 +540,19 @@
 
     mate_core = 1 - me.core
 
+    late = slice(3 * PIECE, T)
+
+    def early(c):
+        right = jnp.concatenate([dg[c, 0, 0 : 3 * PIECE], dg[c, 1, 0 : 3 * PIECE]], 1)
+        first[c] = dot(xb[:, 0 : 3 * PIECE], right)
+
     def multiply(c):
-        right = jnp.concatenate([dg[c, 0], dg[c, 1]], 1)
-        theirs = xb[pl.ds(pl.multiple_of(mate_core * 320, 320), 320), :]
-        core_out[c] = dot(theirs, right).astype(BF16)
+        right = jnp.concatenate([dg[c, 0, late], dg[c, 1, late]], 1)
+        theirs = pl.ds(pl.multiple_of(mate_core * 320, 320), 320)
+        core_out[c] = (first[c, theirs, :] + dot(xb[theirs, late], right)).astype(BF16)
         send(remote(core_out.at[c], core_in.at[c], core_s.at[c], core_r.at[c], me.v, mate))
-        mine = xb[pl.ds(pl.multiple_of(me.core * 320, 320), 320), :]
-        gw[c] = dot(mine, right)
+        mine = pl.ds(pl.multiple_of(me.core * 320, 320), 320)
+        gw[c] = first[c, mine, :] + dot(xb[mine, late], right)
 
     def over_y(c):
         remote(core_out.at[c], core_in.at[c], core_s.at[c], core_r.at[c], me.v, mate).wait_recv()
@@ -597,26 +593,27 @@
         x = lax.rem(me.x + (0, 3, 1, 2)[c], 4)
         grad_weight[:, pl.ds(pl.multiple_of(x * 256, 256), 256)] = total[0:20]
 
+    ask()
     patches(0)
     partials(0)
     start_x(0)
     partials(1)
     start_x(1)
     answer()
+    pass_on(0)
     patches(1)
-    pass_on(0)
-    pass_on(1)
     partials(2)
     start_x(2)
+    pass_on(1)
     partials(3)
     start_x(3)
 
-    first = (me.b + 1) // 2 - 1
+    low_row = (me.b + 1) // 2 - 1
     window[...] = jnp.zeros((LANES, LANES), F32)
     level = iota((45, 16, LANES), 1)
     all_rows = table[...]
-    window[0:45, :] = jnp.sum(jnp.where(level == first, all_rows, 0.0), 1)
-    window[64:109, :] = jnp.sum(jnp.where(level == first + 1, all_rows, 0.0), 1)
+    window[0:45, :] = jnp.sum(jnp.where(level == low_row, all_rows, 0.0), 1)
+    window[64:109, :] = jnp.sum(jnp.where(level == low_row + 1, all_rows, 0.0), 1)
     position = [
         jnp.dot(m.astype(F32), window[...], precision=HI, preferred_element_type=F32)
         for m in mix_blocks(me, False)
@@ -624,7 +621,7 @@
     poscol[...] = jnp.concatenate([posrow[...], jnp.zeros((120, T), F32)], 0).T
 
     finish_x(0)
-    finish_x(1)
+    pass_on(2)
 
     r = iota((640, 1), 0)
 
@@ -642,68 +639,74 @@
     n = 20 * (zl * 8 + y * 2 + core) + r - 20 * zl
     permb[...] = onehot(iota((640, 640), 1) == (n & 7) * 80 + (n >> 3))
 
-    @pl.loop(0, 6)
-    def _(i):
-        xb[:, rows(i, 256)] = dot(permb[...], xt[:, rows(i, 256)]).astype(BF16)
-
-    pass_on(2)
+    def arrange(s):
+        xb[:, sample(s)] = dot(permb[...], xt[:, sample(s)]).astype(BF16)
+
+    arrange(0)
+    finish_x(1)
     pass_on(3)
+    arrange(1)
     place_cot()
+    finish_x(2)
+    finish_z(0)
+    local_sums(0)
+    finish_x(3)
+    finish_z(1)
+    local_sums(1)
+    finish_z(2)
+    local_sums(2)
+    finish_z(3)
+    local_sums(3)
+    norm(0)
+    norm(1)
+    arrange(2)
+    arrange(3)
+    norm(2)
+    norm(3)
+    pass_d(me.h, 0)
+    pass_d(me.h, 1)
+    over_arrives(0)
+    over_arrives(1)
+    pass_d(1 - me.h, 0)
+    pass_d(1 - me.h, 1)
     for i in range(12):
         sl = slice(i * LANES, (i + 1) * LANES)
         slotrow[:, sl] = slotcol[sl, :].T[0:8]
-    finish_z(0)
-    finish_z(1)
-    local_sums(0)
-    finish_x(2)
-    finish_x(3)
-    sums_x(0)
-    sums_z(0)
-    norm(0)
-    finish_z(2)
-    finish_z(3)
-    local_sums(1)
-    over_arrives(0)
-    over_arrives(1)
-    sums_x(1)
-    pass_d(me.h, 0)
-    pass_d(me.h, 1)
-    sums_z(1)
-    norm(1)
-    pass_d(1 - me.h, 0)
-    pass_d(1 - me.h, 1)
     pick_emb()
+    over_arrives(2)
+    pass_d(me.h, 2)
+    early(0)
     table_rows()
-    over_arrives(2)
     over_arrives(3)
+    pass_d(me.h, 3)
     start_emb()
-    pass_d(me.h, 2)
-    pass_d(me.h, 3)
     multiply(0)
+    pass_d(1 - me.h, 2)
+    early(1)
+    over_y(0)
     table_chip()
-    over_y(0)
-    table_z()
-    pass_d(1 - me.h, 2)
+    early(2)
     pass_d(1 - me.h, 3)
-    await_d(1)
     multiply(1)
+    multiply(2)
+    await_d(range(3))
+    early(3)
     over_z(0)
     over_y(1)
+    over_y(2)
+    table_z()
+    await_d(range(3, 4))
+    multiply(3)
+    over_z(1)
+    over_z(2)
+    over_y(3)
     table_y()
-    await_d(2)
-    multiply(2)
-    over_z(1)
-    over_y(2)
+    finish(0)
     place_emb()
-    finish(0)
-    over_z(2)
-    await_d(3)
-    multiply(3)
+    over_z(3)
     finish(1)
-    over_y(3)
     finish(2)
     table_end()
-    over_z(3)
     finish(3)
     for copy in sends:
         copy.wait_send()
@@ -756,18 +759,18 @@
             vmem((PIECE, 640)), vmem((640, E)),
             vmem((4, T, 256)), vmem((T, 256)), vmem((T, 256)), vmem((T, 256)),
             vmem((T, LANES)), vmem((T, LANES)), vmem((LANES, LANES), F32), vmem((T, LANES), F32),
-            vmem((T, LANES), F32), vmem((2, 8, PIECE), F32), vmem((2, 4, 8, PIECE), F32),
-            vmem((2, 8, PIECE), F32), vmem((2, 8, PIECE), F32), vmem((2, PIECE, LANES), F32),
+            vmem((4, 8, 256), F32), vmem((4, NV, 8, 256), F32),
             vmem((T, LANES)), vmem((T, LANES)), vmem((T, LANES)), vmem((4, 2, T, LANES)),
+            vmem((4, 640, 256), F32),
             vmem((4, 320, 256)), vmem((4, 320, 256)), vmem((4, 320, 256), F32),
             vmem((4, 320, 256)), vmem((4, 3, 80, 256)),
             vmem((4, 128, 256)), vmem((4, 3, 32, 256)),
             vmem((48, LANES), F32), vmem((48, LANES), F32), vmem((48, LANES), F32),
             vmem((48, LANES), F32), vmem((48, LANES), F32), vmem((4, 4, 48, LANES), F32),
             dma(5), dma(NB), dma(NB), dma(NB), dma(NB),
-            dma(4), dma(4), dma(4), dma(4), dma(4), dma(4), dma(4), dma(4),
-            dma(2, 3), dma(2, 4), dma(2), dma(2), dma(NB), dma(NB), dma(4), dma(4),
-            dma(2, 4, 2), dma(2, 4), dma(2, 4), dma(2, 4), dma(2, 4),
+            dma(4, 2), dma(4, 2), dma(4, 2), dma(4, 2), dma(4, 2), dma(4, 2), dma(4), dma(4),
+            dma(4, 7), dma(4, NV), dma(NB), dma(NB), dma(4), dma(4),
+            dma(2, 4, 2), dma(2, 4), dma(2, 4), dma(2, 4, 2), dma(2, 4, 2),
             dma(4), dma(4), dma(4, 3), dma(4, 3), dma(4, 3), dma(4, 3),
             dma(2), dma(2), dma(3), dma(3), dma(3), dma(3),
         ],
@@ -777,7 +780,7 @@
         name="encoder",
     )(
         var_ids, var_shift, var_scale, fields, patch_weight.reshape(640, E),
-        pos_table.transpose(1, 0, 2), order.reshape(1, 1440), grad_out,
+        pos_table.transpose(1, 0, 2), order, grad_out,
         layer_norm_gain.reshape(1, LANES), layer_norm_bias.reshape(1, LANES),
     )
     embed, grad_weight, grad_table, grad_gain, grad_bias = pl.pallas_call(

time: 119 us -> 108 us (0.908); the launches traced: 117 us -> 108 us
  Pallas kernels: 115 us -> 108 us
  local copies, waits for them, and re-layouts: 1.29 us -> 0 us
    pallas_call x1, Pallas kernels: 113 us -> 106 us  [on_device(): pl.pallas_call(encoder_kernel, out_shape=out_shape, in_specs=[scalars] *...]
    reshape x1 -> x0, local copies, waits for them, and re-layouts: 1.29 us -> none  [on_device(): order.reshape(1, 1440)]
where the time goes in v3:
time: 108 us
  Pallas kernels  108 us (100%)
    pallas_call x1, Pallas kernels, on_device(): pl.pallas_call(encoder_kernel, out_shape=out_shape, in_specs=[scalars] *...  106 us

profile of v3, /device:TPU:32, one launch (start us, length us, event | category | flops | bytes accessed | tf_op | source)
XLA Modules:
  0.0 108.3 jit_solution(2199083561707894203)
XLA Ops:
  0.6 105.6 %encoder.1 = (bf16[1440,128]{1,0:T(8,128)(2,1)}, f32[20,1024]{1,0:T(8,128)}, f32[45,16,128]{2,1,0:T(8,128)}, f32[1,128]{1,0:T(1,128)}, f32[1,128]{1,0:T(1,128)}) custom-call(s32[10]{0:T(128)} %ids.1, f32[80]{0:T(128)} %shift.1, f32[80]{0:T(128)} %scale.1, bf16[4,10,16,1440]{3,2,1,0:T(8,128)(2,1)} %fields_at.1, bf16[640,1024]{1,0:T(8,128)(2,1)} %bitcast.7, ...), custom_call_target="tpu_custom_call" | custom-call | tf_op jit(solution)/shard_map/encoder/pallas_call | solution.py:747
  106.3 2.1 %results.1 = (bf16[1440,128]{1,0:T(8,128)(2,1)}, f32[20,1024]{1,0:T(8,128)}, f32[45,16,128]{2,1,0:T(8,128)}, f32[1,128]{1,0:T(1,128)}, f32[1,128]{1,0:T(1,128)}) custom-call(bf16[1440,128]{1,0:T(8,128)(2,1)} %get-tuple-element.15.refs_0_, f32[20,1024]{1,0:T(8,128)} %get-tuple-element.16.refs_1_, f32[45,16,128]{2,1,0:T(8,128)} %get-tuple-element.17.refs_2_, ...), custom_call_target="tpu_custom_call" | custom-call | tf_op jit(solution)/shard_map/results/pallas_call | solution.py:786

commit v4 on v3

--- a/solution.py
+++ b/solution.py
@@ -154,9 +154,9 @@
 
 
 def encoder_kernel(
-    ids, shift, scale, fields_at, weight_at, table, order, gout, gain_in, bias_in,
+    ids, shift, scale, fields_at, weight_at, table_at, gout_at, order, gain_in, bias_in,
     embed, grad_weight, grad_table, grad_gain, grad_bias,
-    fields, weight, info, got_info, slotcol, posrow, poscol, slotrow, gpad, cot_out, cot_in, cot,
+    fields, weight, table, info, got_info, slotcol, posrow, poscol, slotrow, gpad, cot_out, cot_in, cot,
     xn, sel, sel_end, perm, permb, xt, xb, xrow, wq, part, leg, from_left, from_right,
     zout, zin, window, pre,
     packed, sums_in, emb, emb_out, emb_in, dg,
@@ -181,6 +181,10 @@
         loads.append(pltpu.make_async_copy(fields_at.at[s], fields.at[s], load_s.at[s]))
     for copy in loads:
         copy.start()
+    gout_load = pltpu.make_async_copy(gout_at, gpad.at[pl.ds(0, 1440)], load_s.at[5])
+    table_load = pltpu.make_async_copy(table_at, table, load_s.at[6])
+    gout_load.start()
+    table_load.start()
 
     info_args = (me, lambda d: info.at[d], lambda s: got_info.at[s], info_s, info_r)
 
@@ -227,16 +231,6 @@
         got_info[pl.ds(me.b, 1)] = info[pl.ds(me.b, 1)]
 
     xn[:, :, :, 1408:1536] = jnp.zeros((2, 4, 80, 128), BF16)
-    for s in range(4):
-        pad = slice(s * PIECE + SENT, (s + 1) * PIECE)
-        zero = jnp.zeros((PIECE - SENT, 256), BF16)
-        from_left[pad, :] = zero
-        from_right[pad, :] = zero
-        zin[pad, :] = zero[:, 0:128]
-        for c in range(4):
-            for hh in range(2):
-                dg[c, hh, pad, :] = zero[:, 0:128]
-
     @pl.loop(0, 8)
     def _(i):
         n = iota((LANES, E), 1)
@@ -258,6 +252,17 @@
         lanes = slice(i * 256, i * 256 + 256)
         wq[:, lanes] = dot(perm[...], weight[:, lanes]).astype(BF16)
     eye = onehot(iota((PIECE, PIECE), 0) == iota((PIECE, PIECE), 1))
+
+    def clear_padding():
+        for s in range(4):
+            pad = slice(s * PIECE + SENT, (s + 1) * PIECE)
+            zero = jnp.zeros((PIECE - SENT, 256), BF16)
+            from_left[pad, :] = zero
+            from_right[pad, :] = zero
+            zin[pad, :] = zero[:, 0:128]
+            for c in range(4):
+                for hh in range(2):
+                    dg[c, hh, pad, :] = zero[:, 0:128]
 
     def patches(ch):
         for s in (2 * ch, 2 * ch + 1):
@@ -356,7 +361,7 @@
 
     def answer():
         gpad[1440:T, :] = jnp.zeros((T - 1440, LANES), BF16)
-        gpad[0:1440, :] = gout[...]
+        gout_load.wait()
         exchange_wait_recv(*info_args)
         asked = jnp.concatenate([got_info[s][0:1] for s in range(NB)], 0)
         asked = jnp.concatenate([asked, jnp.zeros((LANES - NB, LANES), F32)], 0).T
@@ -597,6 +602,7 @@
     patches(0)
     partials(0)
     start_x(0)
+    clear_padding()
     partials(1)
     start_x(1)
     answer()
@@ -611,6 +617,7 @@
     low_row = (me.b + 1) // 2 - 1
     window[...] = jnp.zeros((LANES, LANES), F32)
     level = iota((45, 16, LANES), 1)
+    table_load.wait()
     all_rows = table[...]
     window[0:45, :] = jnp.sum(jnp.where(level == low_row, all_rows, 0.0), 1)
     window[64:109, :] = jnp.sum(jnp.where(level == low_row + 1, all_rows, 0.0), 1)
@@ -747,10 +754,10 @@
     results = pl.pallas_call(
         encoder_kernel,
         out_shape=out_shape,
-        in_specs=[scalars] * 3 + [anywhere] * 2 + [here] * 5,
+        in_specs=[scalars] * 3 + [anywhere] * 4 + [here] * 3,
         out_specs=(here,) * 5,
         scratch_shapes=[
-            vmem((4, 10, 16, 1440)), vmem((640, E)),
+            vmem((4, 10, 16, 1440)), vmem((640, E)), vmem((45, 16, LANES), F32),
             vmem((NB, 8, LANES), F32), vmem((NB, 8, LANES), F32), vmem((T, LANES), F32),
             vmem((8, T), F32), vmem((T, LANES), F32), vmem((8, T), F32),
             vmem((T, LANES)), vmem((T, LANES)), vmem((T, LANES)), vmem((T, LANES)),
@@ -767,7 +774,7 @@
             vmem((4, 128, 256)), vmem((4, 3, 32, 256)),
             vmem((48, LANES), F32), vmem((48, LANES), F32), vmem((48, LANES), F32),
             vmem((48, LANES), F32), vmem((48, LANES), F32), vmem((4, 4, 48, LANES), F32),
-            dma(5), dma(NB), dma(NB), dma(NB), dma(NB),
+            dma(10), dma(NB), dma(NB), dma(NB), dma(NB),
             dma(4, 2), dma(4, 2), dma(4, 2), dma(4, 2), dma(4, 2), dma(4, 2), dma(4), dma(4),
             dma(4, 7), dma(4, NV), dma(NB), dma(NB), dma(4), dma(4),
             dma(2, 4, 2), dma(2, 4), dma(2, 4), dma(2, 4, 2), dma(2, 4, 2),
@@ -780,7 +787,7 @@
         name="encoder",
     )(
         var_ids, var_shift, var_scale, fields, patch_weight.reshape(640, E),
-        pos_table.transpose(1, 0, 2), order, grad_out,
+        pos_table.transpose(1, 0, 2), grad_out, order,
         layer_norm_gain.reshape(1, LANES), layer_norm_bias.reshape(1, LANES),
     )
     embed, grad_weight, grad_table, grad_gain, grad_bias = pl.pallas_call(

time: 108 us -> 107 us (level)
  Pallas kernels: 108 us -> 106 us
    pallas_call x1, Pallas kernels: 106 us -> 104 us  [on_device(): pl.pallas_call(encoder_kernel, out_shape=out_shape, in_specs=[scalars] *...]
where the time goes in v4:
time: 107 us
  Pallas kernels  106 us (99%)
    pallas_call x1, Pallas kernels, on_device(): pl.pallas_call(encoder_kernel, out_shape=out_shape, in_specs=[scalars] *...  104 us

profile of v4, /device:TPU:32, one launch (start us, length us, event | category | flops | bytes accessed | tf_op | source)
XLA Modules:
  0.0 107.0 jit_solution(6906627049893103592)
XLA Ops:
  0.6 104.3 %encoder.1 = (bf16[1440,128]{1,0:T(8,128)(2,1)}, f32[20,1024]{1,0:T(8,128)}, f32[45,16,128]{2,1,0:T(8,128)}, f32[1,128]{1,0:T(1,128)}, f32[1,128]{1,0:T(1,128)}) custom-call(s32[10]{0:T(128)} %ids.1, f32[80]{0:T(128)} %shift.1, f32[80]{0:T(128)} %scale.1, bf16[4,10,16,1440]{3,2,1,0:T(8,128)(2,1)} %fields_at.1, bf16[640,1024]{1,0:T(8,128)(2,1)} %bitcast.7, ...), custom_call_target="tpu_custom_call" | custom-call | tf_op jit(solution)/shard_map/encoder/pallas_call | solution.py:754
  104.9 2.1 %results.1 = (bf16[1440,128]{1,0:T(8,128)(2,1)}, f32[20,1024]{1,0:T(8,128)}, f32[45,16,128]{2,1,0:T(8,128)}, f32[1,128]{1,0:T(1,128)}, f32[1,128]{1,0:T(1,128)}) custom-call(bf16[1440,128]{1,0:T(8,128)(2,1)} %get-tuple-element.15.refs_0_, f32[20,1024]{1,0:T(8,128)} %get-tuple-element.16.refs_1_, f32[45,16,128]{2,1,0:T(8,128)} %get-tuple-element.17.refs_2_, ...), custom_call_target="tpu_custom_call" | custom-call | tf_op jit(solution)/shard_map/results/pallas_call | solution.py:793

commit v5 on v4

--- a/solution.py
+++ b/solution.py
@@ -653,8 +653,8 @@
     finish_x(1)
     pass_on(3)
     arrange(1)
+    finish_x(2)
     place_cot()
-    finish_x(2)
     finish_z(0)
     local_sums(0)
     finish_x(3)

time: 107 us -> 107 us (level)
  no operation moved by 1% of the time
where the time goes in v5:
time: 107 us
  Pallas kernels  106 us (99%)
    pallas_call x1, Pallas kernels, on_device(): pl.pallas_call(encoder_kernel, out_shape=out_shape, in_specs=[scalars] *...  104 us

profile of v5, /device:TPU:32, one launch (start us, length us, event | category | flops | bytes accessed | tf_op | source)
XLA Modules:
  0.0 106.9 jit_solution(2089741055729559206)
XLA Ops:
  0.6 104.2 %encoder.1 = (bf16[1440,128]{1,0:T(8,128)(2,1)}, f32[20,1024]{1,0:T(8,128)}, f32[45,16,128]{2,1,0:T(8,128)}, f32[1,128]{1,0:T(1,128)}, f32[1,128]{1,0:T(1,128)}) custom-call(s32[10]{0:T(128)} %ids.1, f32[80]{0:T(128)} %shift.1, f32[80]{0:T(128)} %scale.1, bf16[4,10,16,1440]{3,2,1,0:T(8,128)(2,1)} %fields_at.1, bf16[640,1024]{1,0:T(8,128)(2,1)} %bitcast.7, ...), custom_call_target="tpu_custom_call" | custom-call | tf_op jit(solution)/shard_map/encoder/pallas_call | solution.py:754
  104.8 2.1 %results.1 = (bf16[1440,128]{1,0:T(8,128)(2,1)}, f32[20,1024]{1,0:T(8,128)}, f32[45,16,128]{2,1,0:T(8,128)}, f32[1,128]{1,0:T(1,128)}, f32[1,128]{1,0:T(1,128)}) custom-call(bf16[1440,128]{1,0:T(8,128)(2,1)} %get-tuple-element.15.refs_0_, f32[20,1024]{1,0:T(8,128)} %get-tuple-element.16.refs_1_, f32[45,16,128]{2,1,0:T(8,128)} %get-tuple-element.17.refs_2_, ...), custom_call_target="tpu_custom_call" | custom-call | tf_op jit(solution)/shard_map/results/pallas_call | solution.py:793
